TPU v7x, 256 devices: a whole 4x4x8 slice. The times are simulated.
256 devices in a mesh: lat: 16 (over x_hi, z), lon: 8 (over y, x_lo), lev: 2 (over core).
Axes of the slice: x: 4 (x_hi: 2, x_lo: 2; x = x_hi * 2 + x_lo), y: 4, z: 8, core: 2. Of those that a mesh axis runs over, the one named last changes fastest.
Arguments:
- tracer: float32 [8, 1024, 2048], P('lev', 'lat', 'lon'), may hold values from -6 to 6
- diffusivity: float32 [8, 1024, 2048], P('lev', 'lat', 'lon'), may hold values from 0.02 to 0.1
- amplitude: float32 [8, 1024, 2048], P('lev', 'lat', 'lon'), may hold values from 0.05 to 0.5
- noise_w: float32 [2, 8, 1024, 2048], P(None, 'lev', 'lat', 'lon'), may hold values from -6 to 6
- noise_z: float32 [2, 8, 1024, 2048], P(None, 'lev', 'lat', 'lon'), may hold values from -6 to 6
- land_sea: int32 [8, 1024, 2048], P('lev', 'lat', 'lon'), may hold values 0 or 1
- partner: int32 [2048], replicated, may hold values from 0 to 2047, as said below
Outputs:
- tracer_out: float32 [8, 1024, 2048], P('lev', 'lat', 'lon')
Inputs may be any that keep to these rules, and one draw needn't show every extreme that they name: partner[i] + i takes the same value modulo 2048 for every column i: the fold is a mirror of the columns.
All inputs are finite; a program needn't handle non-finite values. No bound on the sum of `land_sea` on one device may be relied on, other than what follows from the above.
Results may differ from a plain program's by a relative error of at most 0.00002.
Values sent between devices are 32-bit elements; how exact they have to be, the bound alone decides.
A program may use at most 64 MiB of HBM per device.

v0:
```python
import jax
import jax.numpy as jnp
from jax import lax
from jax.sharding import PartitionSpec as P

STEPS = 2


def padded_2(x, sides, width, wrap):
    for axis, dim in sides:
        size, length = (lax.axis_size(axis), x.shape[dim])
        up = [(i, (i + 1) % size) for i in range(size if wrap else size - 1)]
        down = [(j, i) for i, j in up]
        last = lax.slice_in_dim(x, length - width, length, axis=dim)
        first = lax.slice_in_dim(x, 0, width, axis=dim)
        before = lax.ppermute(last, axis, up)
        after = lax.ppermute(first, axis, down)
        x = jnp.concatenate([before, x, after], axis=dim)
    return x


def extend(stacked, partner, margin):
    row_count = stacked.shape[2]
    col_count = stacked.shape[3]
    rimmed = padded_2(stacked, (("lat", 2), ("lev", 1)), margin, False)
    northern = rimmed[:, :, row_count : row_count + margin, :][:, :, ::-1, :]
    gathered = lax.all_gather(northern, "lon", axis=3, tiled=True)
    all_columns = gathered.shape[3]
    columns = (
        lax.axis_index("lon") * col_count
        - margin
        + jnp.arange(col_count + 2 * margin, dtype=jnp.int32)
    ) % all_columns
    folded = jnp.take(gathered, jnp.take(partner, columns), axis=3)
    padded = padded_2(rimmed, (("lon", 3),), margin, True)
    is_northern = lax.axis_index("lat") == lax.axis_size("lat") - 1
    upper = jnp.where(is_northern, folded, padded[:, :, row_count + margin :, :])
    return padded.at[:, :, row_count + margin :, :].set(upper)


def tendency(values, diffusivity, ocean):
    inner = (slice(1, -1), slice(1, -1), slice(1, -1))
    centre = values[inner]
    centre_diff = diffusivity[inner]
    centre_ocean = ocean[inner]
    summed = jnp.zeros_like(centre)
    for axis_number in range(3):
        for offset in (-1, 1):
            picked = [slice(1, -1), slice(1, -1), slice(1, -1)]
            picked[axis_number] = slice(1 + offset, values.shape[axis_number] - 1 + offset)
            picked = tuple(picked)
            factor = 0.5 if axis_number == 0 else 1.0
            weight = (
                factor * 0.5 * (centre_diff + diffusivity[picked]) * centre_ocean * ocean[picked]
            )
            summed = summed + weight * (values[picked] - centre)
    return summed


def local(tracer, diffusivity, amplitude, noise_w, noise_z, land_sea, partner):
    ocean = land_sea.astype(jnp.float32)
    fixed = extend(jnp.stack([diffusivity, ocean]), partner, 1)
    for step_index in range(STEPS):
        first = tendency(extend(tracer[None], partner, 1)[0], fixed[0], fixed[1])
        section = tracer + 0.75 * first + 1.5 * amplitude * noise_z[step_index]
        second = tendency(extend(section[None], partner, 1)[0], fixed[0], fixed[1])
        tracer = tracer + (first / 3.0 + 2.0 * second / 3.0) + amplitude * noise_w[step_index]
    return tracer


def solution(mesh):
    return jax.shard_map(
        local,
        mesh=mesh,
        in_specs=(
            P("lev", "lat", "lon"),
            P("lev", "lat", "lon"),
            P("lev", "lat", "lon"),
            P(None, "lev", "lat", "lon"),
            P(None, "lev", "lat", "lon"),
            P("lev", "lat", "lon"),
            P(),
        ),
        out_specs=P("lev", "lat", "lon"),
        check_vma=False,
    )
```

profile of v0, /device:TPU:6, one launch (start us, length us, event | category | flops | bytes accessed | tf_op | source)
XLA Modules:
  0.0 264.6 jit_solution(10421656088009430396)
XLA Ops:
  2.1 3.8 %collective-permute-start = (f32[2,4,1,256]{3,0,2,1:T(2,128)S(1)}, f32[2,4,1,256]{3,0,2,1:T(2,128)S(1)}, u32[]{:S(2)}, u32[]{:S(2)}) collective-permute-start(f32[2,4,1,256]{3,0,2,1:T(2,128)S(1)} %copy.302), channel_id=1, source_target_pairs={{0,16},{16,32},{32,48},{48,64},{64,80},{80,96},{96,112},{112,128},... | collective-permute-start | bytes 24584 | tf_op jit(solution)/shard_map/ppermute | solution.py:16
  5.9 6.7 %collective-permute-start.1 = (f32[2,4,1,256]{3,0,2,1:T(2,128)S(1)}, f32[2,4,1,256]{3,0,2,1:T(2,128)S(1)}, u32[]{:S(2)}, u32[]{:S(2)}) collective-permute-start(f32[2,4,1,256]{3,0,2,1:T(2,128)S(1)} %copy.303), channel_id=1, source_target_pairs={{16,0},{32,16},{48,32},{64,48},{80,64},{96,80},{112,96},{128,112},... | collective-permute-start | bytes 24584 | tf_op jit(solution)/shard_map/ppermute | solution.py:17
  12.8 1.9 collective-permute-start.6
  14.8 7.5 %collective-permute-start.7 = (f32[1,4,1,256]{3,1,2,0:T(4,128)S(1)}, f32[1,4,1,256]{3,1,2,0:T(4,128)S(1)}, u32[]{:S(2)}, u32[]{:S(2)}) collective-permute-start(f32[1,4,1,256]{3,1,2,0:T(4,128)S(1)} %get-tuple-element.110), channel_id=1, source_target_pairs={{16,0},{32,16},{48,32},{64,48},{80,64},{96,80},{112,96},{128,112},... | collective-permute-start | bytes 12296 | tf_op jit(solution)/shard_map/ppermute | solution.py:17
  22.3 2.2 gather_fusion.1
  28.7 3.0 %collective-permute-start.2 = (f32[2,1,66,256]{3,0,2,1:T(2,128)}, f32[2,1,66,256]{3,0,2,1:T(2,128)S(1)}, u32[]{:S(2)}, u32[]{:S(2)}) collective-permute-start(f32[2,1,66,256]{3,0,2,1:T(2,128)} %get-tuple-element.83), channel_id=1, source_target_pairs={{0,1},{2,3},{4,5},{6,7},{8,9},{10,11},{12,13},{14,15},{16,17},{18,... | collective-permute-start | bytes 405512 | tf_op jit(solution)/shard_map/ppermute | solution.py:16
  35.4 22.3 %all_gather.16 = f32[1,6,1,2048]{3,2,1,0:T(1,128)S(1)} all-gather(f32[1,6,1,256]{3,2,1,0:T(1,128)S(1)} %slice.566), channel_id=1, replica_groups=mesh['lat'=16,'lon'=8,'lev'=2] {'lon'}, dimensions={3}, use_global_device_ids=true | all-gather | bytes 55296 | tf_op jit(solution)/shard_map/all_gather | solution.py:27
  58.0 1.6 gather_fusion.2
  65.3 35.7 %all_gather.15 = f32[2,6,1,2048]{3,0,2,1:T(2,128)S(1)} all-gather(f32[2,6,1,256]{3,0,2,1:T(2,128)S(1)} %pad_maximum_fusion.20), channel_id=1, replica_groups=mesh['lat'=16,'lon'=8,'lev'=2] {'lon'}, dimensions={3}, use_global_device_ids=true | all-gather | bytes 110592 | tf_op jit(solution)/shard_map/all_gather | solution.py:27
  100.9 2.3 copy.265
  103.3 3.3 %gather_fusion = f32[258,2,6]{2,1,0:T(2,128)} fusion(f32[2,6,2048]{1,0,2:T(2,128)} %bitcast.72, s32[1024]{0:T(1024)S(1)} %pad_clamp_fusion), kind=kCustom, calls=%fused_computation.5 | custom fusion | bytes 25800 | tf_op jit(solution)/shard_map/jit(_take)/gather | solution.py:34
  106.6 2.9 %pad_maximum_fusion = f32[2,6,66,258]{3,0,2,1:T(2,128)S(1)} fusion(f32[2,6,66,1]{3,0,2,1:T(2,128)S(1)} %collective-permute-done.5, f32[2,1,66,256]{3,0,2,1:T(2,128)S(1)} %collective-permute-done.3, f32[2,4,66,256]{3,0,2,1:T(2,128)S(1)} %constant_dynamic-update-slice_fusion, f32[2,1,66,256]{3,0,2,1:T(2,128)S(1)} %collective-permute-done.2, ...), kind=kLoop, calls=%fused_computation.6 | loop fusion | flops 817344 | bytes 1634688 | tf_op jit(solution)/shard_map/concatenate | solution.py:18
  113.8 1.9 collective-permute-start.12
  115.8 7.7 %collective-permute-start.13 = (f32[1,4,1,256]{3,2,1,0:T(1,128)S(1)}, f32[1,4,1,256]{3,2,1,0:T(1,128)S(1)}, u32[]{:S(2)}, u32[]{:S(2)}) collective-permute-start(f32[1,4,1,256]{3,2,1,0:T(1,128)S(1)} %get-tuple-element.108), channel_id=1, source_target_pairs={{16,0},{32,16},{48,32},{64,48},{80,64},{96,80},{112,96},{128,112},... | collective-permute-start | bytes 12296 | tf_op jit(solution)/shard_map/ppermute | solution.py:17
  127.4 1.8 collective-permute-done.15
  130.1 2.8 %collective-permute-start.16 = (f32[1,6,66,1]{3,2,1,0:T(8,128)}, f32[1,6,66,1]{3,2,1,0:T(8,128)S(1)}, u32[]{:S(2)}, u32[]{:S(2)}) collective-permute-start(f32[1,6,66,1]{3,2,1,0:T(8,128)} %get-tuple-element.91), channel_id=1, source_target_pairs={{0,2},{2,4},{4,6},{6,8},{8,10},{10,12},{12,14},{14,0},{1,3},{3,5},... | collective-permute-start | bytes 4760 | tf_op jit(solution)/shard_map/ppermute | solution.py:16
  132.9 23.8 %all_gather.17 = f32[1,6,1,2048]{3,2,1,0:T(1,128)S(1)} all-gather(f32[1,6,1,256]{3,2,1,0:T(1,128)S(1)} %pad_maximum_fusion.23), channel_id=1, replica_groups=mesh['lat'=16,'lon'=8,'lev'=2] {'lon'}, dimensions={3}, use_global_device_ids=true | all-gather | bytes 55296 | tf_op jit(solution)/shard_map/all_gather | solution.py:27
  158.2 2.8 %gather_fusion.3 = f32[258,6]{1,0:T(8,128)} fusion(f32[6,2048]{0,1:T(8,128)} %bitcast.75, s32[1024]{0:T(1024)S(1)} %pad_clamp_fusion), kind=kCustom, calls=%fused_computation.2.clone | custom fusion | bytes 13416 | tf_op jit(solution)/shard_map/jit(_take)/gather | solution.py:34
  164.3 1.5 fusion.32
  165.7 1.9 collective-permute-start.18
  167.7 8.5 %collective-permute-start.19 = (f32[1,4,1,256]{3,2,1,0:T(1,128)S(1)}, f32[1,4,1,256]{3,2,1,0:T(1,128)S(1)}, u32[]{:S(2)}, u32[]{:S(2)}) collective-permute-start(f32[1,4,1,256]{3,2,1,0:T(1,128)S(1)} %get-tuple-element.106), channel_id=1, source_target_pairs={{16,0},{32,16},{48,32},{64,48},{80,64},{96,80},{112,96},{128,112},... | collective-permute-start | bytes 12296 | tf_op jit(solution)/shard_map/ppermute | solution.py:17
  180.3 1.8 collective-permute-done.21
  183.0 2.0 collective-permute-start.23
  185.0 21.4 %all_gather.18 = f32[1,6,1,2048]{3,2,1,0:T(1,128)S(1)} all-gather(f32[1,6,1,256]{3,2,1,0:T(1,128)S(1)} %pad_maximum_fusion.22), channel_id=1, replica_groups=mesh['lat'=16,'lon'=8,'lev'=2] {'lon'}, dimensions={3}, use_global_device_ids=true | all-gather | bytes 55296 | tf_op jit(solution)/shard_map/all_gather | solution.py:27
  210.8 1.5 fusion.66
  212.3 1.9 collective-permute-start.24
  214.3 8.5 %collective-permute-start.25 = (f32[1,4,1,256]{3,2,1,0:T(1,128)S(1)}, f32[1,4,1,256]{3,2,1,0:T(1,128)S(1)}, u32[]{:S(2)}, u32[]{:S(2)}) collective-permute-start(f32[1,4,1,256]{3,2,1,0:T(1,128)S(1)} %get-tuple-element.104), channel_id=1, source_target_pairs={{16,0},{32,16},{48,32},{64,48},{80,64},{96,80},{112,96},{128,112},... | collective-permute-start | bytes 12296 | tf_op jit(solution)/shard_map/ppermute | solution.py:17
  226.9 1.8 collective-permute-done.27
  229.8 1.8 collective-permute-start.29
  231.6 23.3 %all_gather.19 = f32[1,6,1,2048]{3,2,1,0:T(1,128)S(1)} all-gather(f32[1,6,1,256]{3,2,1,0:T(1,128)S(1)} %pad_maximum_fusion.21), channel_id=1, replica_groups=mesh['lat'=16,'lon'=8,'lev'=2] {'lon'}, dimensions={3}, use_global_device_ids=true | all-gather | bytes 55296 | tf_op jit(solution)/shard_map/all_gather | solution.py:27
  256.3 2.8 %gather_fusion.5 = f32[258,6]{1,0:T(8,128)} fusion(f32[6,2048]{0,1:T(8,128)} %bitcast.73, s32[1024]{0:T(1024)S(1)} %pad_clamp_fusion), kind=kCustom, calls=%fused_computation.4.clone | custom fusion | bytes 13416 | tf_op jit(solution)/shard_map/jit(_take)/gather | solution.py:34
  262.4 2.2 fusion.6
  (150 shorter events, 48.6 us)
Async XLA Ops:
  0.0 22.3 %copy-start = (s32[2048]{0:T(1024)S(1)}, s32[2048]{0:T(1024)}, u32[]{:S(2)}) copy-start(s32[2048]{0:T(1024)} %param.27) | copy-start | bytes 24580
  2.1 25.4 %collective-permute-start = (f32[2,4,1,256]{3,0,2,1:T(2,128)S(1)}, f32[2,4,1,256]{3,0,2,1:T(2,128)S(1)}, u32[]{:S(2)}, u32[]{:S(2)}) collective-permute-start(f32[2,4,1,256]{3,0,2,1:T(2,128)S(1)} %copy.302), channel_id=1, source_target_pairs={{0,16},{16,32},{32,48},{48,64},{64,80},{80,96},{96,112},{112,128},... | collective-permute-start | bytes 24584 | tf_op jit(solution)/shard_map/ppermute | solution.py:16
  5.9 22.0 %collective-permute-start.1 = (f32[2,4,1,256]{3,0,2,1:T(2,128)S(1)}, f32[2,4,1,256]{3,0,2,1:T(2,128)S(1)}, u32[]{:S(2)}, u32[]{:S(2)}) collective-permute-start(f32[2,4,1,256]{3,0,2,1:T(2,128)S(1)} %copy.303), channel_id=1, source_target_pairs={{16,0},{32,16},{48,32},{64,48},{80,64},{96,80},{112,96},{128,112},... | collective-permute-start | bytes 24584 | tf_op jit(solution)/shard_map/ppermute | solution.py:17
  12.8 11.8 %collective-permute-start.6 = (f32[1,4,1,256]{3,1,2,0:T(4,128)S(1)}, f32[1,4,1,256]{3,1,2,0:T(4,128)S(1)}, u32[]{:S(2)}, u32[]{:S(2)}) collective-permute-start(f32[1,4,1,256]{3,1,2,0:T(4,128)S(1)} %get-tuple-element.109), channel_id=1, source_target_pairs={{0,16},{16,32},{32,48},{48,64},{64,80},{80,96},{96,112},{112,128},... | collective-permute-start | bytes 12296 | tf_op jit(solution)/shard_map/ppermute | solution.py:16
  14.8 9.9 %collective-permute-start.7 = (f32[1,4,1,256]{3,1,2,0:T(4,128)S(1)}, f32[1,4,1,256]{3,1,2,0:T(4,128)S(1)}, u32[]{:S(2)}, u32[]{:S(2)}) collective-permute-start(f32[1,4,1,256]{3,1,2,0:T(4,128)S(1)} %get-tuple-element.110), channel_id=1, source_target_pairs={{16,0},{32,16},{48,32},{64,48},{80,64},{96,80},{112,96},{128,112},... | collective-permute-start | bytes 12296 | tf_op jit(solution)/shard_map/ppermute | solution.py:17
  24.6 137.7 %copy-start.8 = (pred[258]{0:T(512)(128)(4,1)}, pred[258]{0:T(512)(128)(4,1)S(1)}, u32[]{:S(2)}) copy-start(pred[258]{0:T(512)(128)(4,1)S(1)} %get-tuple-element.77) | copy-start | bytes 778
  24.8 8.2 %collective-permute-start.8 = (f32[1,1,66,256]{3,1,2,0:T(1,128)S(1)}, f32[1,1,66,256]{3,1,2,0:T(1,128)S(1)}, u32[]{:S(2)}, u32[]{:S(2)}) collective-permute-start(f32[1,1,66,256]{3,1,2,0:T(1,128)S(1)} %get-tuple-element.102), channel_id=1, source_target_pairs={{0,1},{2,3},{4,5},{6,7},{8,9},{10,11},{12,13},{14,15},{16,17},{18,... | collective-permute-start | bytes 202760 | tf_op jit(solution)/shard_map/ppermute | solution.py:16
  26.1 7.0 %collective-permute-start.9 = (f32[1,1,66,256]{3,1,2,0:T(1,128)S(1)}, f32[1,1,66,256]{3,1,2,0:T(1,128)S(1)}, u32[]{:S(2)}, u32[]{:S(2)}) collective-permute-start(f32[1,1,66,256]{3,1,2,0:T(1,128)S(1)} %get-tuple-element.101), channel_id=1, source_target_pairs={{1,0},{3,2},{5,4},{7,6},{9,8},{11,10},{13,12},{15,14},{17,16},{19,... | collective-permute-start | bytes 202760 | tf_op jit(solution)/shard_map/ppermute | solution.py:17
  28.7 32.6 %collective-permute-start.2 = (f32[2,1,66,256]{3,0,2,1:T(2,128)}, f32[2,1,66,256]{3,0,2,1:T(2,128)S(1)}, u32[]{:S(2)}, u32[]{:S(2)}) collective-permute-start(f32[2,1,66,256]{3,0,2,1:T(2,128)} %get-tuple-element.83), channel_id=1, source_target_pairs={{0,1},{2,3},{4,5},{6,7},{8,9},{10,11},{12,13},{14,15},{16,17},{18,... | collective-permute-start | bytes 405512 | tf_op jit(solution)/shard_map/ppermute | solution.py:16
  31.8 29.6 %collective-permute-start.3 = (f32[2,1,66,256]{3,0,2,1:T(2,128)}, f32[2,1,66,256]{3,0,2,1:T(2,128)S(1)}, u32[]{:S(2)}, u32[]{:S(2)}) collective-permute-start(f32[2,1,66,256]{3,0,2,1:T(2,128)} %get-tuple-element.84), channel_id=1, source_target_pairs={{1,0},{3,2},{5,4},{7,6},{9,8},{11,10},{13,12},{15,14},{17,16},{19,... | collective-permute-start | bytes 405512 | tf_op jit(solution)/shard_map/ppermute | solution.py:17
  33.3 27.3 %collective-permute-start.10 = (f32[1,6,66,1]{3,2,1,0:T(8,128)S(1)}, f32[1,6,66,1]{3,2,1,0:T(8,128)S(1)}, u32[]{:S(2)}, u32[]{:S(2)}) collective-permute-start(f32[1,6,66,1]{3,2,1,0:T(8,128)S(1)} %get-tuple-element.93), channel_id=1, source_target_pairs={{0,2},{2,4},{4,6},{6,8},{8,10},{10,12},{12,14},{14,0},{1,3},{3,5},... | collective-permute-start | bytes 4760 | tf_op jit(solution)/shard_map/ppermute | solution.py:16
  34.3 26.3 %collective-permute-start.11 = (f32[1,6,66,1]{3,2,1,0:T(8,128)S(1)}, f32[1,6,66,1]{3,2,1,0:T(8,128)S(1)}, u32[]{:S(2)}, u32[]{:S(2)}) collective-permute-start(f32[1,6,66,1]{3,2,1,0:T(8,128)S(1)} %get-tuple-element.94), channel_id=1, source_target_pairs={{2,0},{4,2},{6,4},{8,6},{10,8},{12,10},{14,12},{0,14},{3,1},{5,3},... | collective-permute-start | bytes 4760 | tf_op jit(solution)/shard_map/ppermute | solution.py:17
  63.1 43.5 %collective-permute-start.4 = (f32[2,6,66,1]{3,0,2,1:T(2,128)}, f32[2,6,66,1]{3,0,2,1:T(2,128)S(1)}, u32[]{:S(2)}, u32[]{:S(2)}) collective-permute-start(f32[2,6,66,1]{3,0,2,1:T(2,128)} %get-tuple-element.81), channel_id=1, source_target_pairs={{0,2},{2,4},{4,6},{6,8},{8,10},{10,12},{12,14},{14,0},{1,3},{3,5},... | collective-permute-start | bytes 9512 | tf_op jit(solution)/shard_map/ppermute | solution.py:16
  64.0 42.6 %collective-permute-start.5 = (f32[2,6,66,1]{3,0,2,1:T(2,128)S(1)}, f32[2,6,66,1]{3,0,2,1:T(2,128)S(1)}, u32[]{:S(2)}, u32[]{:S(2)}) collective-permute-start(f32[2,6,66,1]{3,0,2,1:T(2,128)S(1)} %get-tuple-element.82), channel_id=1, source_target_pairs={{2,0},{4,2},{6,4},{8,6},{10,8},{12,10},{14,12},{0,14},{3,1},{5,3},... | collective-permute-start | bytes 9512 | tf_op jit(solution)/shard_map/ppermute | solution.py:17
  113.8 9.7 %collective-permute-start.12 = (f32[1,4,1,256]{3,2,1,0:T(1,128)S(1)}, f32[1,4,1,256]{3,2,1,0:T(1,128)S(1)}, u32[]{:S(2)}, u32[]{:S(2)}) collective-permute-start(f32[1,4,1,256]{3,2,1,0:T(1,128)S(1)} %get-tuple-element.107), channel_id=1, source_target_pairs={{0,16},{16,32},{32,48},{48,64},{64,80},{80,96},{96,112},{112,128},... | collective-permute-start | bytes 12296 | tf_op jit(solution)/shard_map/ppermute | solution.py:16
  115.8 8.8 %collective-permute-start.13 = (f32[1,4,1,256]{3,2,1,0:T(1,128)S(1)}, f32[1,4,1,256]{3,2,1,0:T(1,128)S(1)}, u32[]{:S(2)}, u32[]{:S(2)}) collective-permute-start(f32[1,4,1,256]{3,2,1,0:T(1,128)S(1)} %get-tuple-element.108), channel_id=1, source_target_pairs={{16,0},{32,16},{48,32},{64,48},{80,64},{96,80},{112,96},{128,112},... | collective-permute-start | bytes 12296 | tf_op jit(solution)/shard_map/ppermute | solution.py:17
  124.7 2.7 %collective-permute-start.14 = (f32[1,1,66,256]{3,1,2,0:T(1,128)S(1)}, f32[1,1,66,256]{3,1,2,0:T(1,128)S(1)}, u32[]{:S(2)}, u32[]{:S(2)}) collective-permute-start(f32[1,1,66,256]{3,1,2,0:T(1,128)S(1)} %copy.275), channel_id=1, source_target_pairs={{0,1},{2,3},{4,5},{6,7},{8,9},{10,11},{12,13},{14,15},{16,17},{18,... | collective-permute-start | bytes 202760 | tf_op jit(solution)/shard_map/ppermute | solution.py:16
  126.1 3.2 %collective-permute-start.15 = (f32[1,1,66,256]{3,1,2,0:T(1,128)S(1)}, f32[1,1,66,256]{3,1,2,0:T(1,128)S(1)}, u32[]{:S(2)}, u32[]{:S(2)}) collective-permute-start(f32[1,1,66,256]{3,1,2,0:T(1,128)S(1)} %copy.276), channel_id=1, source_target_pairs={{1,0},{3,2},{5,4},{7,6},{9,8},{11,10},{13,12},{15,14},{17,16},{19,... | collective-permute-start | bytes 202760 | tf_op jit(solution)/shard_map/ppermute | solution.py:17
  130.1 31.8 %collective-permute-start.16 = (f32[1,6,66,1]{3,2,1,0:T(8,128)}, f32[1,6,66,1]{3,2,1,0:T(8,128)S(1)}, u32[]{:S(2)}, u32[]{:S(2)}) collective-permute-start(f32[1,6,66,1]{3,2,1,0:T(8,128)} %get-tuple-element.91), channel_id=1, source_target_pairs={{0,2},{2,4},{4,6},{6,8},{8,10},{10,12},{12,14},{14,0},{1,3},{3,5},... | collective-permute-start | bytes 4760 | tf_op jit(solution)/shard_map/ppermute | solution.py:16
  132.9 29.1 %collective-permute-start.17 = (f32[1,6,66,1]{3,2,1,0:T(8,128)S(1)}, f32[1,6,66,1]{3,2,1,0:T(8,128)S(1)}, u32[]{:S(2)}, u32[]{:S(2)}) collective-permute-start(f32[1,6,66,1]{3,2,1,0:T(8,128)S(1)} %get-tuple-element.92), channel_id=1, source_target_pairs={{2,0},{4,2},{6,4},{8,6},{10,8},{12,10},{14,12},{0,14},{3,1},{5,3},... | collective-permute-start | bytes 4760 | tf_op jit(solution)/shard_map/ppermute | solution.py:17
  165.7 10.4 %collective-permute-start.18 = (f32[1,4,1,256]{3,2,1,0:T(1,128)S(1)}, f32[1,4,1,256]{3,2,1,0:T(1,128)S(1)}, u32[]{:S(2)}, u32[]{:S(2)}) collective-permute-start(f32[1,4,1,256]{3,2,1,0:T(1,128)S(1)} %get-tuple-element.105), channel_id=1, source_target_pairs={{0,16},{16,32},{32,48},{48,64},{64,80},{80,96},{96,112},{112,128},... | collective-permute-start | bytes 12296 | tf_op jit(solution)/shard_map/ppermute | solution.py:16
  167.7 9.8 %collective-permute-start.19 = (f32[1,4,1,256]{3,2,1,0:T(1,128)S(1)}, f32[1,4,1,256]{3,2,1,0:T(1,128)S(1)}, u32[]{:S(2)}, u32[]{:S(2)}) collective-permute-start(f32[1,4,1,256]{3,2,1,0:T(1,128)S(1)} %get-tuple-element.106), channel_id=1, source_target_pairs={{16,0},{32,16},{48,32},{64,48},{80,64},{96,80},{112,96},{128,112},... | collective-permute-start | bytes 12296 | tf_op jit(solution)/shard_map/ppermute | solution.py:17
  177.6 2.7 %collective-permute-start.20 = (f32[1,1,66,256]{3,1,2,0:T(1,128)S(1)}, f32[1,1,66,256]{3,1,2,0:T(1,128)S(1)}, u32[]{:S(2)}, u32[]{:S(2)}) collective-permute-start(f32[1,1,66,256]{3,1,2,0:T(1,128)S(1)} %copy.281), channel_id=1, source_target_pairs={{0,1},{2,3},{4,5},{6,7},{8,9},{10,11},{12,13},{14,15},{16,17},{18,... | collective-permute-start | bytes 202760 | tf_op jit(solution)/shard_map/ppermute | solution.py:16
  179.0 3.2 %collective-permute-start.21 = (f32[1,1,66,256]{3,1,2,0:T(1,128)S(1)}, f32[1,1,66,256]{3,1,2,0:T(1,128)S(1)}, u32[]{:S(2)}, u32[]{:S(2)}) collective-permute-start(f32[1,1,66,256]{3,1,2,0:T(1,128)S(1)} %copy.282), channel_id=1, source_target_pairs={{1,0},{3,2},{5,4},{7,6},{9,8},{11,10},{13,12},{15,14},{17,16},{19,... | collective-permute-start | bytes 202760 | tf_op jit(solution)/shard_map/ppermute | solution.py:17
  183.0 24.9 %collective-permute-start.22 = (f32[1,6,66,1]{3,2,1,0:T(8,128)}, f32[1,6,66,1]{3,2,1,0:T(8,128)}, u32[]{:S(2)}, u32[]{:S(2)}) collective-permute-start(f32[1,6,66,1]{3,2,1,0:T(8,128)} %get-tuple-element.89), channel_id=1, source_target_pairs={{0,2},{2,4},{4,6},{6,8},{8,10},{10,12},{12,14},{14,0},{1,3},{3,5},... | collective-permute-start | bytes 4760 | tf_op jit(solution)/shard_map/ppermute | solution.py:16
  183.0 24.9 %collective-permute-start.23 = (f32[1,6,66,1]{3,2,1,0:T(8,128)}, f32[1,6,66,1]{3,2,1,0:T(8,128)}, u32[]{:S(2)}, u32[]{:S(2)}) collective-permute-start(f32[1,6,66,1]{3,2,1,0:T(8,128)} %get-tuple-element.90), channel_id=1, source_target_pairs={{2,0},{4,2},{6,4},{8,6},{10,8},{12,10},{14,12},{0,14},{3,1},{5,3},... | collective-permute-start | bytes 4760 | tf_op jit(solution)/shard_map/ppermute | solution.py:17
  212.3 10.4 %collective-permute-start.24 = (f32[1,4,1,256]{3,2,1,0:T(1,128)S(1)}, f32[1,4,1,256]{3,2,1,0:T(1,128)S(1)}, u32[]{:S(2)}, u32[]{:S(2)}) collective-permute-start(f32[1,4,1,256]{3,2,1,0:T(1,128)S(1)} %get-tuple-element.103), channel_id=1, source_target_pairs={{0,16},{16,32},{32,48},{48,64},{64,80},{80,96},{96,112},{112,128},... | collective-permute-start | bytes 12296 | tf_op jit(solution)/shard_map/ppermute | solution.py:16
  214.3 9.8 %collective-permute-start.25 = (f32[1,4,1,256]{3,2,1,0:T(1,128)S(1)}, f32[1,4,1,256]{3,2,1,0:T(1,128)S(1)}, u32[]{:S(2)}, u32[]{:S(2)}) collective-permute-start(f32[1,4,1,256]{3,2,1,0:T(1,128)S(1)} %get-tuple-element.104), channel_id=1, source_target_pairs={{16,0},{32,16},{48,32},{64,48},{80,64},{96,80},{112,96},{128,112},... | collective-permute-start | bytes 12296 | tf_op jit(solution)/shard_map/ppermute | solution.py:17
  224.2 2.7 %collective-permute-start.26 = (f32[1,1,66,256]{3,1,2,0:T(1,128)S(1)}, f32[1,1,66,256]{3,1,2,0:T(1,128)S(1)}, u32[]{:S(2)}, u32[]{:S(2)}) collective-permute-start(f32[1,1,66,256]{3,1,2,0:T(1,128)S(1)} %copy.287), channel_id=1, source_target_pairs={{0,1},{2,3},{4,5},{6,7},{8,9},{10,11},{12,13},{14,15},{16,17},{18,... | collective-permute-start | bytes 202760 | tf_op jit(solution)/shard_map/ppermute | solution.py:16
  225.6 3.2 %collective-permute-start.27 = (f32[1,1,66,256]{3,1,2,0:T(1,128)S(1)}, f32[1,1,66,256]{3,1,2,0:T(1,128)S(1)}, u32[]{:S(2)}, u32[]{:S(2)}) collective-permute-start(f32[1,1,66,256]{3,1,2,0:T(1,128)S(1)} %copy.288), channel_id=1, source_target_pairs={{1,0},{3,2},{5,4},{7,6},{9,8},{11,10},{13,12},{15,14},{17,16},{19,... | collective-permute-start | bytes 202760 | tf_op jit(solution)/shard_map/ppermute | solution.py:17
  229.6 30.5 %collective-permute-start.28 = (f32[1,6,66,1]{3,2,1,0:T(8,128)}, f32[1,6,66,1]{3,2,1,0:T(8,128)S(1)}, u32[]{:S(2)}, u32[]{:S(2)}) collective-permute-start(f32[1,6,66,1]{3,2,1,0:T(8,128)} %get-tuple-element.87), channel_id=1, source_target_pairs={{0,2},{2,4},{4,6},{6,8},{8,10},{10,12},{12,14},{14,0},{1,3},{3,5},... | collective-permute-start | bytes 4760 | tf_op jit(solution)/shard_map/ppermute | solution.py:16
  229.8 30.4 %collective-permute-start.29 = (f32[1,6,66,1]{3,2,1,0:T(8,128)S(1)}, f32[1,6,66,1]{3,2,1,0:T(8,128)S(1)}, u32[]{:S(2)}, u32[]{:S(2)}) collective-permute-start(f32[1,6,66,1]{3,2,1,0:T(8,128)S(1)} %get-tuple-element.88), channel_id=1, source_target_pairs={{2,0},{4,2},{6,4},{8,6},{10,8},{12,10},{14,12},{0,14},{3,1},{5,3},... | collective-permute-start | bytes 4760 | tf_op jit(solution)/shard_map/ppermute | solution.py:17
  (9 other events, 26.5 us)
where the time goes:
time: 266 us; the launch traced here: 265 us
  blocking collectives  126 us (47%)
  starting transfers between devices  76.3 us (29%)
  local copies, waits for them, and re-layouts  31.5 us (12%)
  other arithmetic  20.2 us (8%)
  waiting for transfers between devices  9.29 us (3%)
    all_gather x5, blocking collectives, extend(): gathered = lax.all_gather(northern, 'lon', axis=3, tiled=True)  126 us
    ppermute x15, starting transfers between devices, padded_2(): after = lax.ppermute(first, axis, down)  51.7 us
    ppermute x15, starting transfers between devices, padded_2(): before = lax.ppermute(last, axis, up)  24.7 us
    gather x10, local copies, waits for them, and re-layouts, extend(): folded = jnp.take(gathered, jnp.take(partner, columns), axis=3)  16.8 us
    ppermute x15, waiting for transfers between devices, padded_2(): after = lax.ppermute(first, axis, down)  9.26 us
    concatenate x10, other arithmetic, padded_2(): x = jnp.concatenate([before, x, after], axis=dim)  5.77 us
  transfers between devices with their start and end apart: 30, of which 6 were waited for; matrix products, arithmetic and copies ran while one was open for 10% of the time, Pallas kernels for 0%

commit v1 on v0

v1 whole, which is shorter than its diff:
```python
import jax
import jax.numpy as jnp
from jax import lax
from jax.experimental import pallas as pl
from jax.experimental.pallas import tpu as pltpu
from jax.sharding import PartitionSpec as P


LAT, LON, LEV = 16, 8, 2
NL, ROWS, COLS = 4, 64, 256
RT = ROWS // 8
VMEM = 63 * 1024 * 1024
MESH = pl.DeviceIdType.MESH
f32 = jnp.float32


def kernel(
    tracer, diff, amp, noise_w, noise_z, land, partner, out,
    rx, rd, ra, rl, rw, rz, pc,
    xe, me, ge, he, ae, ke, x1, k2, wx, wy, wz, mp, mr,
    na, sa, nb, sb, em, wm, dne, dnw, dse, dsw, fa, fb,
    tn1, ts1, tn2, ts2, ep, wp, dn, ds,
    isem, ssem, rsem, fsem_s, fsem_r,
):
    lat, lon, lev = lax.axis_index("lat"), lax.axis_index("lon"), lax.axis_index("lev")
    east, west = lax.rem(lon + 1, LON), lax.rem(lon + LON - 1, LON)
    other = 1 - lev
    north_in, south_in = lat < LAT - 1, lat > 0
    at_fold = lat == LAT - 1

    bar = pltpu.get_barrier_semaphore()

    def greet(**where):
        pl.semaphore_signal(bar, inc=1, device_id=where, device_id_type=MESH)

    @pl.when(north_in)
    def _():
        greet(lat=lat + 1)
        greet(lat=lat + 1, lon=east)
        greet(lat=lat + 1, lon=west)

    @pl.when(south_in)
    def _():
        greet(lat=lat - 1)
        greet(lat=lat - 1, lon=east)
        greet(lat=lat - 1, lon=west)

    greet(lon=east)
    greet(lon=west)

    @pl.when(at_fold)
    def _():
        for k in range(2, LON - 1):
            greet(lon=lax.rem(lon + k, LON))

    greet(lev=other)

    loads = [
        pltpu.make_async_copy(s, d, isem.at[k])
        for k, (s, d) in enumerate(
            ((tracer, rx), (diff, rd), (land, rl), (amp, ra), (noise_z, rz), (noise_w, rw), (partner, pc))
        )
    ]
    for c in loads:
        c.start()

    lane = lax.broadcasted_iota(jnp.int32, (8, 128), 1)
    sub = lax.broadcasted_iota(jnp.int32, (8, 128), 0)
    lo_half, lo_sub = lane < 64, sub < 4
    east_part = (lane & 4) != 0

    def lroll(v, s):
        s = s % 128
        return v if s == 0 else pltpu.roll(v, s, 1)

    def sroll(v, s):
        return pltpu.roll(v, s, 0)

    def closed(v):
        return jnp.where(v > 0, v, -1.0)

    zero = jnp.zeros((8, 128), f32)
    own = NL * lev + 1

    def outside(r, _):
        sl = pl.ds(pl.multiple_of(8 * r, 8), 8)
        for p in (0, 9):
            for lt in range(3):
                me[p, lt, sl, :] = zero - 1.0
                for ref in (xe, ke, x1, k2):
                    ref[p, lt, sl, :] = zero
        return 0

    lax.fori_loop(0, RT + 1, outside, 0)

    @pl.when(lat == 0)
    def _():
        for i in range(NL):
            for lt in range(3):
                sa[NL * lev + i, lt] = zero
                sb[NL * lev + i, lt] = zero

    for c in loads:
        c.wait()

    def prep(n, _):
        i, r = n // RT, n % RT
        sl = pl.ds(pl.multiple_of(8 * r, 8), 8)
        p = own + i
        for lt in range(2):
            cs = pl.ds(128 * lt, 128)
            x = rx[i, sl, cs]
            amp_ = ra[i, sl, cs]
            m = 0.5 * rd[i, sl, cs] * rl[i, sl, cs].astype(f32)
            xe[p, lt, sl, :] = x
            mp[i, lt, sl, :] = m
            me[p, lt, sl, :] = closed(m)
            ge[p, lt, sl, :] = x + amp_ * rz[0, i, sl, cs]
            he[p, lt, sl, :] = x + amp_ * rw[0, i, sl, cs]
            ae[p, lt, sl, :] = amp_ * rz[1, i, sl, cs]
        return 0

    lax.fori_loop(0, NL * RT, prep, 0)

    def first_rows(x, m):
        return jnp.where(lo_sub, x, sroll(m, 4))

    def first_rows2(g, h, a):
        return jnp.where(lo_sub, g, jnp.where(sub == 7, sroll(a, 7), sroll(h, 4)))

    def last_rows(x, m):
        return jnp.where(lo_sub, sroll(m, 4), x)

    def last_rows2(g, h, a):
        return jnp.where(lo_sub, jnp.where(sub == 0, sroll(a, 1), sroll(h, 4)), g)

    top, bottom = pl.ds(ROWS - 8, 8), pl.ds(0, 8)

    def pack_rows(i, _):
        p = own + i
        for lt in range(2):
            tn1[i, lt] = first_rows(xe[p, lt, bottom, :], mp[i, lt, bottom, :])
            tn2[i, lt] = first_rows2(ge[p, lt, bottom, :], he[p, lt, bottom, :], ae[p, lt, bottom, :])
            ts1[i, lt] = last_rows(xe[p, lt, top, :], mp[i, lt, top, :])
            ts2[i, lt] = last_rows2(ge[p, lt, top, :], he[p, lt, top, :], ae[p, lt, top, :])
        return 0

    lax.fori_loop(0, NL, pack_rows, 0)

    for one, two, dst in ((tn1, tn2, dn), (ts1, ts2, ds)):
        d = zero
        for i in range(NL):
            z1 = jnp.where(lo_half, one[i, 0], one[i, 1])
            z2 = jnp.where(lo_half, two[i, 0], two[i, 1])
            d = jnp.where((lane >> 3) == 2 * i, lroll(z1, 16 * i + 4), d)
            d = jnp.where((lane >> 3) == 2 * i + 1, lroll(z2, 16 * i + 12), d)
        dst[...] = d

    def pack_columns(i, _):
        p = own + i
        p1, p2 = zero, zero
        for r in range(RT):
            sl = pl.ds(8 * r, 8)

            def edge(ref, q):
                return jnp.where(lo_half, ref[q, 0, sl, :], ref[q, 1, sl, :])

            a = edge(ae, p)
            ha = jnp.where(
                lane == 3, lroll(a, 3), jnp.where(lane == 124, lroll(a, 125), edge(he, p))
            )
            p1 = jnp.where((lane >> 3) == 2 * r, lroll(edge(xe, p), 16 * r + 4), p1)
            p1 = jnp.where((lane >> 3) == 2 * r + 1, lroll(edge(mp, i), 16 * r + 12), p1)
            at = (lane + 128 - 4 - 16 * r) & 127
            p2 = jnp.where(at < 8, lroll(edge(ge, p), 16 * r + 8), p2)
            p2 = jnp.where((at >= 8) & (at < 16), lroll(ha, 16 * r + 16), p2)
        ep[i] = jnp.where(east_part, p1, p2)
        wp[i] = jnp.where(east_part, p2, p1)
        return 0

    lax.fori_loop(0, NL, pack_columns, 0)

    def mirror_rows(v):
        for b in (1, 2, 4):
            v = jnp.where((sub & b) != 0, sroll(v, b), sroll(v, 8 - b))
        return v

    def mirror_lanes(v):
        for b in (1, 2, 4, 8, 16, 32, 64):
            v = jnp.where((lane & b) != 0, lroll(v, b), lroll(v, 128 - b))
        return v

    @pl.when(at_fold)
    def _():
        def pack_fold(i, _):
            p = own + i
            for lt in range(2):
                x, m, g, h, a = (
                    mirror_rows(v)
                    for v in (
                        xe[p, lt, top, :], mp[i, lt, top, :], ge[p, lt, top, :],
                        he[p, lt, top, :], ae[p, lt, top, :],
                    )
                )
                fa[2 * lon + lt, i] = mirror_lanes(first_rows(x, m))
                fb[2 * lon + lt, i] = mirror_lanes(first_rows2(g, h, a))
            return 0

        lax.fori_loop(0, NL, pack_fold, 0)

    @pl.when(lat == 0)
    def _():
        pl.semaphore_wait(bar, 6)

    @pl.when(at_fold)
    def _():
        pl.semaphore_wait(bar, 6 + LON - 3)

    @pl.when(north_in & south_in)
    def _():
        pl.semaphore_wait(bar, 9)

    def send(k, src, dst, **where):
        return pltpu.make_async_remote_copy(
            src_ref=src, dst_ref=dst, send_sem=ssem.at[k], recv_sem=rsem.at[k],
            device_id=where, device_id_type=MESH,
        )

    mine = pl.ds(NL * lev, NL)
    up, down = jnp.minimum(lat + 1, LAT - 1), jnp.maximum(lat - 1, 0)
    to_south = [
        send(0, tn1, na.at[mine, pl.ds(0, 2)], lat=down),
        send(1, dn, dne, lat=down, lon=west),
        send(2, dn, dnw, lat=down, lon=east),
        send(3, tn2, nb.at[mine, pl.ds(0, 2)], lat=down),
    ]
    to_north = [
        send(4, ts1, sa.at[mine, pl.ds(0, 2)], lat=up),
        send(5, ds, dse, lat=up, lon=west),
        send(6, ds, dsw, lat=up, lon=east),
        send(7, ts2, sb.at[mine, pl.ds(0, 2)], lat=up),
    ]
    to_side = [
        send(8, ep, em.at[mine], lon=west),
        send(9, wp, wm.at[mine], lon=east),
    ]
    block = pl.ds(2 * lon, 2)

    def fold_send(ref, half, k):
        return pltpu.make_async_remote_copy(
            src_ref=ref.at[block], dst_ref=ref.at[block],
            send_sem=fsem_s.at[half, k - 1], recv_sem=fsem_r.at[half, k - 1],
            device_id={"lon": lax.rem(lon + k, LON)}, device_id_type=MESH,
        )

    to_fold = [[fold_send(ref, half, k) for k in range(1, LON)] for half, ref in enumerate((fa, fb))]

    @pl.when(south_in)
    def _():
        for c in to_south[:3]:
            c.start()

    @pl.when(north_in)
    def _():
        for c in to_north[:3]:
            c.start()

    @pl.when(at_fold)
    def _():
        for c in to_fold[0]:
            c.start()

    for c in to_side:
        c.start()

    @pl.when(south_in)
    def _():
        to_south[3].start()

    @pl.when(north_in)
    def _():
        to_north[3].start()

    @pl.when(at_fold)
    def _():
        for c in to_fold[1]:
            c.start()

    inner = (pl.ds(0, 2), pl.ds(0, ROWS))

    def planes(ref, start, count):
        return ref.at[(pl.ds(start, count),) + inner]

    to_core = [
        send(10, planes(xe, own, NL), planes(xe, own, NL), lev=other),
        send(11, mp, mr, lev=other),
        send(12, planes(ge, 2 + 3 * lev, 3), planes(ge, 2 + 3 * lev, 3), lev=other),
        send(13, planes(he, 3 + 2 * lev, 2), planes(he, 3 + 2 * lev, 2), lev=other),
        send(14, planes(ae, 4 + lev, 1), planes(ae, 4 + lev, 1), lev=other),
    ]
    for c in to_core:
        c.start()

    def arrived(ref, start, count, k):
        part = planes(ref, start, count)
        pltpu.make_async_remote_copy(
            src_ref=part, dst_ref=part, send_sem=ssem.at[k], recv_sem=rsem.at[k],
            device_id={"lev": other}, device_id_type=MESH,
        ).wait_recv()

    theirs = NL * other + 1
    arrived(xe, theirs, NL, 10)
    to_core[1].wait_recv()
    arrived(ge, 2 + 3 * other, 3, 12)
    arrived(he, 3 + 2 * other, 2, 13)
    arrived(ae, 4 + other, 1, 14)

    def close(n, _):
        i, r = n // RT, n % RT
        sl = pl.ds(pl.multiple_of(8 * r, 8), 8)
        for lt in range(2):
            me[theirs + i, lt, sl, :] = closed(mr[i, lt, sl, :])
        return 0

    lax.fori_loop(0, NL * RT, close, 0)

    def relay(k, ref, start, count):
        part = ref.at[pl.ds(start, count)]
        return send(k, part, part, lev=other)

    relays = [
        relay(15, em, NL * lev, NL),
        relay(16, wm, NL * lev, NL),
        relay(17, na, NL * lev, NL),
        relay(18, sa, NL * lev, NL),
        relay(19, nb, 1 + 3 * lev, 3),
        relay(20, sb, 1 + 3 * lev, 3),
    ]
    to_side[0].wait_recv()
    relays[0].start()
    to_side[1].wait_recv()
    relays[1].start()

    def corners(e_ref, w_ref, one, two):
        d = jnp.where(east_part, e_ref[...], w_ref[...])
        for i in range(NL):
            one[NL * lev + i, 2] = lroll(d, 128 - (16 * i + 4))
            two[NL * lev + i, 2] = lroll(d, 128 - (16 * i + 12))

    @pl.when(south_in)
    def _():
        for c in to_north[:3]:
            c.wait_recv()
        corners(dse, dsw, sa, sb)

    relays[3].start()

    c0 = (pc[0] - COLS * lon) & (LON * COLS - 1)
    t0, shift = c0 >> 7, c0 & 127

    def unfold(src, dst):
        def level(i, _):
            t = [src[(t0 + k) & (2 * LON - 1), i] for k in (-3, -2, -1, 0, 1)]
            v = [
                pltpu.roll(jnp.where(lane >= 127 - shift, t[k + 1], t[k]), (shift + 1) & 127, 1)
                for k in range(4)
            ]
            dst[NL * lev + i, 0] = v[2]
            dst[NL * lev + i, 1] = v[1]
            dst[NL * lev + i, 2] = jnp.where(lo_half, v[0], v[3])
            return 0

        lax.fori_loop(0, NL, level, 0)

    def fold_arrived(ref, half):
        for k in range(1, LON):
            slot = pl.ds(2 * lax.rem(lon + LON - k, LON), 2)
            pltpu.make_async_remote_copy(
                src_ref=ref.at[slot], dst_ref=ref.at[slot],
                send_sem=fsem_s.at[half, k - 1], recv_sem=fsem_r.at[half, k - 1],
                device_id={"lon": lax.rem(lon + k, LON)}, device_id_type=MESH,
            ).wait_recv()

    @pl.when(north_in)
    def _():
        for c in to_south[:3]:
            c.wait_recv()
        corners(dne, dnw, na, nb)

    @pl.when(at_fold)
    def _():
        fold_arrived(fa, 0)
        unfold(fa, na)

    relays[2].start()

    @pl.when(south_in)
    def _():
        to_north[3].wait_recv()

    relays[5].start()

    @pl.when(north_in)
    def _():
        to_south[3].wait_recv()

    @pl.when(at_fold)
    def _():
        fold_arrived(fb, 1)
        unfold(fb, nb)

    relays[4].start()

    def relayed(k, ref, start, count):
        relay(k, ref, start, count).wait_recv()

    relayed(15, em, NL * other, NL)
    relayed(16, wm, NL * other, NL)
    relayed(17, na, NL * other, NL)
    relayed(18, sa, NL * other, NL)
    relayed(19, nb, 1 + 3 * other, 3)
    relayed(20, sb, 1 + 3 * other, 3)

    ring = pl.ds(ROWS, 8)

    def place_first(l, _):
        p = l + 1
        c1 = jnp.where(east_part, em[l], wm[l])
        for r in range(RT):
            sl = pl.ds(8 * r, 8)
            xe[p, 2, sl, :] = lroll(c1, 128 - (16 * r + 4))
            me[p, 2, sl, :] = closed(lroll(c1, 128 - (16 * r + 12)))
        for lt in range(3):
            n, s = na[l, lt], sa[l, lt]
            xe[p, lt, ring, :] = jnp.where(lo_sub, n, s)
            me[p, lt, ring, :] = closed(sroll(jnp.where(lo_sub, s, n), 4))
        return 0

    lax.fori_loop(0, 2 * NL, place_first, 0)

    def place_second(j, _):
        l = j + lev
        p = l + 1
        c2 = jnp.where(east_part, wm[l], em[l])
        for r in range(RT):
            sl = pl.ds(8 * r, 8)
            ge[p, 2, sl, :] = lroll(c2, 128 - (16 * r + 8))
            ha = lroll(c2, 128 - (16 * r + 16))
            he[p, 2, sl, :] = ha
            ae[p, 2, sl, :] = jnp.where(lo_half, lroll(ha, 125), lroll(ha, 3))
        for lt in range(3):
            n, s = nb[l, lt], sb[l, lt]
            ge[p, lt, ring, :] = jnp.where(lo_sub, n, s)
            ha = sroll(jnp.where(lo_sub, s, n), 4)
            he[p, lt, ring, :] = ha
            ae[p, lt, ring, :] = jnp.where(lo_sub, sroll(ha, 5), sroll(ha, 3))
        return 0

    lax.fori_loop(0, 2 * NL - 1, place_second, 0)

    def east_of(v):
        rolled = [lroll(t, 127) for t in v]
        return [jnp.where(lane == 127, rolled[(k + 1) % 3], rolled[k]) for k in range(3)]

    def west_of(v):
        rolled = [lroll(t, 1) for t in v]
        return [jnp.where(lane == 0, rolled[(k + 2) % 3], rolled[k]) for k in range(3)]

    def rows(ref, p, r):
        sl = pl.ds(8 * (r % (RT + 1)), 8)
        return [ref[p, lt, sl, :] for lt in range(3)]

    def weights(j, _):
        p = j + lev + 1
        nxt = [sroll(t, 7) for t in rows(me, p, 0)]
        first = nxt
        for r in range(RT + 1):
            sl = pl.ds(8 * r, 8)
            here, here_up = rows(me, p, r), nxt
            nxt = [sroll(t, 7) for t in rows(me, p, r + 1)] if r < RT else first
            e = east_of(here)
            below = rows(me, p - 1, r)
            for lt in range(3):
                n = jnp.where(sub == 7, nxt[lt], here_up[lt])
                wx[p, lt, sl, :] = jnp.maximum(here[lt] + e[lt], 0.0)
                wy[p, lt, sl, :] = jnp.maximum(here[lt] + n, 0.0)
                wz[p, lt, sl, :] = jnp.maximum(0.5 * (here[lt] + below[lt]), 0.0)
        return 0

    lax.fori_loop(0, 2 * NL, weights, 0)

    def operator(u, p, finish, last):
        def north_flux(r, up_here, up_next):
            here, w = rows(u, p, r), rows(wy, p, r)
            return [
                w[k] * (jnp.where(sub == 7, up_next[k], up_here[k]) - here[k]) for k in range(3)
            ]

        first = [sroll(t, 7) for t in rows(u, p, 0)]
        end = [sroll(t, 7) for t in rows(u, p, RT)]
        before = [sroll(t, 1) for t in north_flux(RT, end, first)]
        up_here = first
        for r in range(RT if last else RT + 1):
            if r + 1 < RT:
                up_next = [sroll(t, 7) for t in rows(u, p, r + 1)]
            else:
                up_next = end if r + 1 == RT else first
            here = rows(u, p, r)
            fy = north_flux(r, up_here, up_next)
            fy_up = [sroll(t, 1) for t in fy]
            e, w = east_of(here), rows(wx, p, r)
            fx = [w[k] * (e[k] - here[k]) for k in range(3)]
            fw = west_of(fx)
            above, below = rows(u, p + 1, r), rows(u, p - 1, r)
            wa, wb = rows(wz, p + 1, r), rows(wz, p, r)
            for k in range(2 if last else 3):
                fs = jnp.where(sub == 0, before[k], fy_up[k])
                total = (
                    (fx[k] - fw[k])
                    + (fy[k] - fs)
                    + (wa[k] * (above[k] - here[k]) - wb[k] * (here[k] - below[k]))
                )
                finish(r, k, total)
            before, up_here = fy_up, up_next

    def stage1(j, _):
        p = 1 + j + lev

        def finish(r, k, total):
            sl = pl.ds(8 * r, 8)
            ke[p, k, sl, :] = ge[p, k, sl, :] + 0.5 * total

        operator(xe, p, finish, False)
        return 0

    def stage2(j, _):
        p = 1 + j + 2 * lev

        def finish(r, k, total):
            sl = pl.ds(8 * r, 8)
            x1[p, k, sl, :] = he[p, k, sl, :] + total

        operator(ke, p, finish, False)
        return 0

    def stage3(j, _):
        p = 1 + j + 3 * lev

        def finish(r, k, total):
            sl = pl.ds(8 * r, 8)
            k2[p, k, sl, :] = (x1[p, k, sl, :] + ae[p, k, sl, :]) + 0.5 * total

        operator(x1, p, finish, False)
        return 0

    def stage4(j, _):
        p = 1 + j + 4 * lev

        def finish(r, k, total):
            sl, cs = pl.ds(8 * r, 8), pl.ds(128 * k, 128)
            out[j, sl, cs] = (x1[p, k, sl, :] + ra[j, sl, cs] * rw[1, j, sl, cs]) + total

        operator(k2, p, finish, True)
        return 0

    lax.fori_loop(0, 7, stage1, 0)
    lax.fori_loop(0, 6, stage2, 0)
    lax.fori_loop(0, 5, stage3, 0)
    lax.fori_loop(0, 4, stage4, 0)

    for c in to_side + to_core + relays:
        c.wait_send()

    @pl.when(south_in)
    def _():
        for c in to_south:
            c.wait_send()

    @pl.when(north_in)
    def _():
        for c in to_north:
            c.wait_send()

    @pl.when(at_fold)
    def _():
        for half in to_fold:
            for c in half:
                c.wait_send()


def local(tracer, diffusivity, amplitude, noise_w, noise_z, land_sea, partner):
    def vm(*shape, dtype=f32):
        return pltpu.VMEM(shape, dtype)

    cells = (NL, ROWS, COLS)
    plane = (3, ROWS + 8, 128)
    tile = (8, 128)
    rim = (2 * NL, 3) + tile
    sides = (2 * NL,) + tile
    rows = (NL, 2) + tile
    return pl.pallas_call(
        kernel,
        out_shape=jax.ShapeDtypeStruct(cells, f32),
        in_specs=[pl.BlockSpec(memory_space=pltpu.HBM)] * 7,
        out_specs=pl.BlockSpec(memory_space=pltpu.VMEM),
        scratch_shapes=[
            vm(*cells), vm(*cells), vm(*cells), vm(*cells, dtype=jnp.int32), vm(2, *cells), vm(2, *cells),
            pltpu.SMEM((LON * COLS,), jnp.int32),
        ]
        + [vm(10, *plane)] * 11
        + [vm(NL, 2, ROWS, 128)] * 2
        + [vm(*rim)] * 4
        + [vm(*sides)] * 2
        + [vm(*tile)] * 4
        + [vm(2 * LON, NL, *tile)] * 2
        + [vm(*rows)] * 4
        + [vm(NL, *tile)] * 2
        + [vm(*tile)] * 2
        + [
            pltpu.SemaphoreType.DMA((7,)),
            pltpu.SemaphoreType.DMA((21,)),
            pltpu.SemaphoreType.DMA((21,)),
            pltpu.SemaphoreType.DMA((2, LON - 1)),
            pltpu.SemaphoreType.DMA((2, LON - 1)),
        ],
        compiler_params=pltpu.CompilerParams(
            collective_id=0, has_side_effects=True, vmem_limit_bytes=VMEM
        ),
        name="ocean",
    )(tracer, diffusivity, amplitude, noise_w, noise_z, land_sea, partner)


def solution(mesh):
    block = P("lev", "lat", "lon")
    steps = P(None, "lev", "lat", "lon")
    return jax.shard_map(
        local,
        mesh=mesh,
        in_specs=(block, block, block, steps, steps, block, P()),
        out_specs=block,
        check_vma=False,
    )
```

time: 266 us -> 26.7 us (0.10)
  the two profiles are of different devices: /device:TPU:6 before, /device:TPU:229 now
where the time goes in v1:
time: 26.7 us; the launch traced here: 26.5 us
  Pallas kernels  24.9 us (93%)
  local copies, waits for them, and re-layouts  1.67 us (6%)
    pallas_call x1, Pallas kernels, local(): pl.pallas_call(kernel, out_shape=jax.ShapeDtypeStruct(cells, f32), in_spe...  24.9 us
    unnamed x1, local copies, waits for them, and re-layouts  1.67 us

profile of v1, /device:TPU:229, one launch (start us, length us, event | category | flops | bytes accessed | tf_op | source)
XLA Modules:
  0.0 26.5 jit_solution(15207046413020582887)
XLA Ops:
  0.0 24.9 %ocean.1 = f32[4,64,256]{2,1,0:T(8,128)} custom-call(f32[4,64,256]{2,1,0:T(8,128)} %tracer.1, f32[4,64,256]{2,1,0:T(8,128)} %diff.1, f32[4,64,256]{2,1,0:T(8,128)} %amp.1, f32[2,4,64,256]{3,2,1,0:T(8,128)} %noise_w.1, f32[2,4,64,256]{3,2,1,0:T(8,128)} %noise_z.1, s32[4,64,256]{2,1,0:T(8,128)} %land.1, s32[2048]{0:T(1024)} %partner.1), custom_call_target="tpu_custom_call" | custom-call | tf_op jit(solution)/shard_map/ocean/pallas_call | solution.py:601
  24.9 1.7 %copy.9 = f32[4,64,256]{2,1,0:T(8,128)} copy(f32[4,64,256]{2,1,0:T(8,128)} %ocean.1) | data formatting | bytes 524288

commit v2 on v0

v2 whole, which is shorter than its diff:
```python
import jax
import jax.numpy as jnp
from jax import lax
from jax.experimental import pallas as pl
from jax.experimental.pallas import tpu as pltpu
from jax.sharding import PartitionSpec as P


LAT, LON, LEV = 16, 8, 2
NL, ROWS, COLS = 4, 64, 256
RT = ROWS // 8
VMEM = 60 * 1024 * 1024
MESH = pl.DeviceIdType.MESH
f32 = jnp.float32
X, M, G, H, A = range(5)


def kernel(
    tracer, diff, amp, noise_w, noise_z, land, partner, out,
    rx, rd, ra, rl, rw, rz, pc,
    xe, me, ge, he, ae, ke, x1, k2, wx, wy, wz, mp, mr, so,
    bx, bm, bg, bh, ba, vx, vy, vz, kr, x1r, k2r, x2r,
    na, sa, nb, sb, em, wm, dne, dnw, dse, dsw, fa, fb,
    tn1, ts1, tn2, ts2, ep, wp, dn, ds,
    isem, ssem, rsem, fsem_s, fsem_r,
):
    lat, lon, lev = lax.axis_index("lat"), lax.axis_index("lon"), lax.axis_index("lev")
    east, west = lax.rem(lon + 1, LON), lax.rem(lon + LON - 1, LON)
    other = 1 - lev
    north_in, south_in = lat < LAT - 1, lat > 0
    at_fold = lat == LAT - 1
    own, theirs = NL * lev + 1, NL * other + 1

    bar = pltpu.get_barrier_semaphore()

    def greet(**where):
        pl.semaphore_signal(bar, inc=1, device_id=where, device_id_type=MESH)

    @pl.when(north_in)
    def _():
        greet(lat=lat + 1)
        greet(lat=lat + 1, lon=east)
        greet(lat=lat + 1, lon=west)

    @pl.when(south_in)
    def _():
        greet(lat=lat - 1)
        greet(lat=lat - 1, lon=east)
        greet(lat=lat - 1, lon=west)

    greet(lon=east)
    greet(lon=west)

    @pl.when(at_fold)
    def _():
        for k in range(2, LON - 1):
            greet(lon=lax.rem(lon + k, LON))

    greet(lev=other)

    loads = [
        pltpu.make_async_copy(s, d, isem.at[k])
        for k, (s, d) in enumerate(
            ((tracer, rx), (diff, rd), (land, rl), (amp, ra), (noise_z, rz), (noise_w, rw), (partner, pc))
        )
    ]
    for c in loads:
        c.start()

    lane = lax.broadcasted_iota(jnp.int32, (8, 128), 1)
    sub = lax.broadcasted_iota(jnp.int32, (8, 128), 0)
    lo_half, lo_sub = lane < 64, sub < 4
    group_e = (lane * 171) >> 11
    group_w = (((lane + 8) * 171) >> 11) - 1
    k12 = lane - 12 * group_e
    halo_e, halo_w = k12 >= 8, (k12 >= 4) & (k12 < 8)
    ring_e = (group_e == 0) | (group_e == RT + 1)
    ring_w = (group_w == 0) | (group_w == RT + 1)
    zero = jnp.zeros((8, 128), f32)
    where = jnp.where

    def lroll(v, s):
        s = s % 128
        return v if s == 0 else pltpu.roll(v, s, 1)

    def sroll(v, s):
        return pltpu.roll(v, s, 0)

    def closed(v):
        return where(v > 0, v, -1.0)

    def both(v):
        return where(lo_half, v[0], v[1])

    top, bottom = pl.ds(ROWS - 8, 8), pl.ds(0, 8)

    def rows_at(r):
        return pl.ds(pl.multiple_of(8 * r, 8), 8)

    for c in loads[:3]:
        c.wait()

    def prep_first(i, _):
        p = own + i
        for r in range(RT):
            sl = pl.ds(8 * r, 8)
            for lt in range(2):
                cs = pl.ds(128 * lt, 128)
                m = 0.5 * rd[i, sl, cs] * rl[i, sl, cs].astype(f32)
                xe[p, lt, sl, :] = rx[i, sl, cs]
                mp[i, lt, sl, :] = m
                me[p, lt, sl, :] = closed(m)
        return 0

    lax.fori_loop(0, NL, prep_first, 0)

    def first_rows(x, m):
        return where(lo_sub, x, sroll(m, 4))

    def first_rows2(g, h, a):
        return where(lo_sub, g, where(sub == 7, sroll(a, 7), sroll(h, 4)))

    def last_rows(x, m):
        return where(lo_sub, sroll(m, 4), x)

    def last_rows2(g, h, a):
        return where(lo_sub, where(sub == 0, sroll(a, 1), sroll(h, 4)), g)

    def mirror_rows(v):
        for b in (1, 2, 4):
            v = where((sub & b) != 0, sroll(v, b), sroll(v, 8 - b))
        return v

    def mirror_lanes(v):
        return jnp.take_along_axis(v, 127 - lane, axis=1, mode="promise_in_bounds")

    for i in range(NL):
        for lt in range(2):
            tn1[i, lt] = first_rows(xe[own + i, lt, bottom, :], mp[i, lt, bottom, :])
            ts1[i, lt] = last_rows(xe[own + i, lt, top, :], mp[i, lt, top, :])

    @pl.when(at_fold)
    def _():
        for i in range(NL):
            for lt in range(2):
                x, m = mirror_rows(xe[own + i, lt, top, :]), mirror_rows(mp[i, lt, top, :])
                fa[2 * lon + lt, i] = mirror_lanes(first_rows(x, m))

    @pl.when(lat == 0)
    def _():
        pl.semaphore_wait(bar, 6)

    @pl.when(at_fold)
    def _():
        pl.semaphore_wait(bar, 6 + LON - 3)

    @pl.when(north_in & south_in)
    def _():
        pl.semaphore_wait(bar, 9)

    def send(k, src, dst, **where):
        return pltpu.make_async_remote_copy(
            src_ref=src, dst_ref=dst, send_sem=ssem.at[k], recv_sem=rsem.at[k],
            device_id=where, device_id_type=MESH,
        )

    mine = pl.ds(NL * lev, NL)
    two = pl.ds(0, 2)
    up, down = jnp.minimum(lat + 1, LAT - 1), jnp.maximum(lat - 1, 0)
    to_south = [
        send(0, tn1, na.at[mine, two], lat=down),
        send(1, tn2, nb.at[mine, two], lat=down),
        send(2, dn, dne, lat=down, lon=west),
        send(3, dn, dnw, lat=down, lon=east),
    ]
    to_north = [
        send(4, ts1, sa.at[mine, two], lat=up),
        send(5, ts2, sb.at[mine, two], lat=up),
        send(6, ds, dse, lat=up, lon=west),
        send(7, ds, dsw, lat=up, lon=east),
    ]
    to_side = [
        send(8, ep, em.at[mine], lon=west),
        send(9, wp, wm.at[mine], lon=east),
    ]
    block = pl.ds(2 * lon, 2)

    def fold_copy(ref, slot, half, k):
        return pltpu.make_async_remote_copy(
            src_ref=ref.at[slot], dst_ref=ref.at[slot],
            send_sem=fsem_s.at[half, k - 1], recv_sem=fsem_r.at[half, k - 1],
            device_id={"lon": lax.rem(lon + k, LON)}, device_id_type=MESH,
        )

    to_fold = [
        [fold_copy(ref, block, half, k) for k in range(1, LON)] for half, ref in enumerate((fa, fb))
    ]

    def planes(ref, start, count):
        return ref.at[pl.ds(start, count)]

    def share(k, ref, start, count):
        part = planes(ref, start, count)
        return send(k, part, part, lev=other)

    @pl.when(south_in)
    def _():
        to_south[0].start()

    @pl.when(north_in)
    def _():
        to_north[0].start()

    @pl.when(at_fold)
    def _():
        for c in to_fold[0]:
            c.start()

    to_core = [share(10, xe, own, NL), send(11, mp, mr, lev=other)]
    for c in to_core:
        c.start()

    for c in loads[3:]:
        c.wait()

    def prep_second(i, _):
        p = own + i
        for r in range(RT):
            sl = pl.ds(8 * r, 8)
            for lt in range(2):
                cs = pl.ds(128 * lt, 128)
                x = rx[i, sl, cs]
                amp_ = ra[i, sl, cs]
                ge[p, lt, sl, :] = x + amp_ * rz[0, i, sl, cs]
                he[p, lt, sl, :] = x + amp_ * rw[0, i, sl, cs]
                ae[p, lt, sl, :] = amp_ * rz[1, i, sl, cs]
        return 0

    lax.fori_loop(0, NL, prep_second, 0)

    for i in range(NL):
        p = own + i
        for lt in range(2):
            tn2[i, lt] = first_rows2(ge[p, lt, bottom, :], he[p, lt, bottom, :], ae[p, lt, bottom, :])
            ts2[i, lt] = last_rows2(ge[p, lt, top, :], he[p, lt, top, :], ae[p, lt, top, :])

    @pl.when(at_fold)
    def _():
        for i in range(NL):
            p = own + i
            for lt in range(2):
                g, h, a = (mirror_rows(ref[p, lt, top, :]) for ref in (ge, he, ae))
                fb[2 * lon + lt, i] = mirror_lanes(first_rows2(g, h, a))

    @pl.when(south_in)
    def _():
        to_south[1].start()

    @pl.when(north_in)
    def _():
        to_north[1].start()

    @pl.when(at_fold)
    def _():
        for c in to_fold[1]:
            c.start()

    for halves, dst in (((tn1, tn2), dn), ((ts1, ts2), ds)):
        d = zero
        for i in range(NL):
            for n, half in enumerate(halves):
                k = 2 * i + n
                d = where((lane >> 3) == k, lroll(both(half[i]), 8 * k + 4), d)
        dst[...] = d

    @pl.when(south_in)
    def _():
        to_south[2].start()
        to_south[3].start()

    @pl.when(north_in)
    def _():
        to_north[2].start()
        to_north[3].start()

    def pack_strips(i, _):
        p = own + i
        strips = []
        for f, ref, q in ((X, xe, p), (M, mp, i), (G, ge, p), (H, he, p), (A, ae, p)):
            s_e, s_w = zero, zero
            for r in range(RT):
                sl = pl.ds(8 * r, 8)
                v = lroll(where(lo_half, ref[q, 0, sl, :], ref[q, 1, sl, :]), 12 * (r + 1) + 8)
                s_e = where(group_e == r + 1, v, s_e)
                s_w = where(group_w == r + 1, v, s_w)
            so[p - 1, f, 0] = s_e
            so[p - 1, f, 1] = s_w
            strips.append(s_e)
        x, m, g, h, a = strips
        ep[i, 0] = where(halo_e, x, where(halo_w, lroll(m, 124), lroll(g, 120)))
        ep[i, 1] = where(halo_e, h, lroll(a, 124))
        wp[i, 0] = where(halo_w, x, where(halo_e, lroll(m, 4), lroll(g, 124)))
        wp[i, 1] = where(halo_w, h, lroll(a, 4))
        return 0

    lax.fori_loop(0, NL, pack_strips, 0)
    for c in to_side:
        c.start()

    late = [
        share(12, ge, 2 + 3 * lev, 3),
        share(13, he, 3 + 2 * lev, 2),
        share(14, ae, 4 + lev, 1),
        share(15, so, NL * lev, NL),
    ]
    for c in late:
        c.start()
    to_core += late

    for p in (0, 9):
        for lt in range(2):
            for r in range(RT):
                sl = pl.ds(8 * r, 8)
                me[p, lt, sl, :] = zero - 1.0
                for ref in (xe, ke, x1, k2):
                    ref[p, lt, sl, :] = zero
        for k in range(4):
            bx[p, k] = zero
            bm[p, k] = zero - 1.0
        for k in range(8):
            for ref in (kr, x1r, k2r):
                ref[p, k] = zero

    @pl.when(lat == 0)
    def _():
        for i in range(NL):
            for lt in range(3):
                sa[NL * lev + i, lt] = zero
                sb[NL * lev + i, lt] = zero

    share(10, xe, theirs, NL).wait_recv()
    to_core[1].wait_recv()

    def close(i, _):
        for r in range(RT):
            sl = pl.ds(8 * r, 8)
            for lt in range(2):
                me[theirs + i, lt, sl, :] = closed(mr[i, lt, sl, :])
        return 0

    lax.fori_loop(0, NL, close, 0)

    def pair(ref, p, r):
        sl = pl.ds(8 * r, 8)
        return [ref[p, lt, sl, :] for lt in range(2)]

    def east_of(v):
        r0, r1 = lroll(v[0], 127), lroll(v[1], 127)
        return [where(lane == 127, r1, r0), r1]

    def west_of(v):
        r0, r1 = lroll(v[0], 1), lroll(v[1], 1)
        return [r0, where(lane == 0, r0, r1)]

    def weights(j, _):
        p = j + lev + 1
        nxt = [sroll(t, 7) for t in pair(me, p, 0)]
        for r in range(RT):
            sl = pl.ds(8 * r, 8)
            here, here_up = pair(me, p, r), nxt
            if r + 1 < RT:
                nxt = [sroll(t, 7) for t in pair(me, p, r + 1)]
            e = east_of(here)
            below = pair(me, p - 1, r)
            for lt in range(2):
                n = where(sub == 7, nxt[lt], here_up[lt])
                wx[p, lt, sl, :] = jnp.maximum(here[lt] + e[lt], 0.0)
                wy[p, lt, sl, :] = jnp.maximum(here[lt] + n, 0.0)
                wz[p, lt, sl, :] = jnp.maximum(0.5 * (here[lt] + below[lt]), 0.0)
        return 0

    lax.fori_loop(0, 2 * NL, weights, 0)

    def inner(u, p, finish):
        up_here = [sroll(t, 7) for t in pair(u, p, 0)]
        before = [zero, zero]
        for r in range(RT):
            up_next = [sroll(t, 7) for t in pair(u, p, r + 1)] if r + 1 < RT else up_here
            here = pair(u, p, r)
            w = pair(wy, p, r)
            fy = [w[k] * (where(sub == 7, up_next[k], up_here[k]) - here[k]) for k in range(2)]
            fy_up = [sroll(t, 1) for t in fy]
            e, w = east_of(here), pair(wx, p, r)
            fx = [w[k] * (e[k] - here[k]) for k in range(2)]
            fw = west_of(fx)
            above, below = pair(u, p + 1, r), pair(u, p - 1, r)
            wa, wb = pair(wz, p + 1, r), pair(wz, p, r)
            for k in range(2):
                fs = where(sub == 0, before[k], fy_up[k])
                total = (
                    (fx[k] - fw[k])
                    + (fy[k] - fs)
                    + (wa[k] * (above[k] - here[k]) - wb[k] * (here[k] - below[k]))
                )
                finish(pl.ds(8 * r, 8), k, total)
            before, up_here = fy_up, up_next

    def inner1(j, _):
        p = 1 + j + lev

        def finish(sl, k, total):
            ke[p, k, sl, :] = ge[p, k, sl, :] + 0.5 * total

        inner(xe, p, finish)
        return 0

    def inner2(j, _):
        p = 1 + j + 2 * lev

        def finish(sl, k, total):
            x1[p, k, sl, :] = he[p, k, sl, :] + total

        inner(ke, p, finish)
        return 0

    def inner3(j, _):
        p = 1 + j + 3 * lev

        def finish(sl, k, total):
            k2[p, k, sl, :] = (x1[p, k, sl, :] + ae[p, k, sl, :]) + 0.5 * total

        inner(x1, p, finish)
        return 0

    def inner4(j, _):
        p = own + j

        def finish(sl, k, total):
            cs = pl.ds(128 * k, 128)
            out[j, sl, cs] = (x1[p, k, sl, :] + ra[j, sl, cs] * rw[1, j, sl, cs]) + total

        inner(k2, p, finish)
        return 0

    share(12, ge, 2 + 3 * other, 3).wait_recv()
    lax.fori_loop(0, 7, inner1, 0)
    share(13, he, 3 + 2 * other, 2).wait_recv()
    lax.fori_loop(0, 6, inner2, 0)
    share(14, ae, 4 + other, 1).wait_recv()
    lax.fori_loop(0, 5, inner3, 0)
    lax.fori_loop(0, 4, inner4, 0)
    share(15, so, NL * other, NL).wait_recv()

    relays = [
        share(16, em, NL * lev, NL),
        share(17, wm, NL * lev, NL),
        share(18, na, NL * lev, NL),
        share(19, sa, NL * lev, NL),
        share(20, nb, 1 + 3 * lev, 3),
        share(21, sb, 1 + 3 * lev, 3),
    ]
    to_side[0].wait_recv()
    relays[0].start()
    to_side[1].wait_recv()
    relays[1].start()

    def corners(w_ref, e_ref, at, one, half2):
        d = where((lane & 4) == 0, w_ref[...], e_ref[...])
        for i in range(NL):
            one[NL * lev + i, 2] = lroll(d, at - 16 * i)
            half2[NL * lev + i, 2] = lroll(d, at - 16 * i - 8)

    @pl.when(south_in)
    def _():
        for k in (0, 2, 3):
            to_north[k].wait_recv()
        corners(dsw, dse, 4, sa, sb)

    relays[3].start()

    c0 = (pc[0] - COLS * lon) & (LON * COLS - 1)
    t0, shift = c0 >> 7, c0 & 127

    def unfold(src, dst):
        for i in range(NL):
            t = [src[(t0 + k) & (2 * LON - 1), i] for k in (-3, -2, -1, 0, 1)]
            v = [
                pltpu.roll(where(lane >= 127 - shift, t[k + 1], t[k]), (shift + 1) & 127, 1)
                for k in range(4)
            ]
            dst[NL * lev + i, 0] = v[2]
            dst[NL * lev + i, 1] = v[1]
            dst[NL * lev + i, 2] = lroll(where(lo_half, v[0], v[3]), 116)

    def fold_arrived(ref, half):
        for k in range(1, LON):
            slot = pl.ds(2 * lax.rem(lon + LON - k, LON), 2)
            fold_copy(ref, slot, half, k).wait_recv()

    @pl.when(north_in)
    def _():
        for k in (0, 2, 3):
            to_south[k].wait_recv()
        corners(dnw, dne, 112, na, nb)

    @pl.when(at_fold)
    def _():
        fold_arrived(fa, 0)
        unfold(fa, na)

    relays[2].start()

    @pl.when(south_in)
    def _():
        to_north[1].wait_recv()

    relays[5].start()

    @pl.when(north_in)
    def _():
        to_south[1].wait_recv()

    @pl.when(at_fold)
    def _():
        fold_arrived(fb, 1)
        unfold(fb, nb)

    relays[4].start()

    def ends(n, s):
        r = where(lo_half, lroll(both(s), 8), lroll(both(n), 116))
        c = where(lo_half, s[2], n[2])
        return where(halo_e, c, r), where(halo_w, c, r)

    def strip(l, f, v_e, v_w, from_e, from_w):
        return (
            where(ring_e, v_e, where(halo_e, from_e, so[l, f, 0])),
            where(ring_w, v_w, where(halo_w, from_w, so[l, f, 1])),
        )

    def place_first(l):
        p = l + 1
        n, s = [na[l, k] for k in range(3)], [sa[l, k] for k in range(3)]
        e1, w1 = em[l, 0], wm[l, 0]
        for lt in range(2):
            bx[p, lt] = where(lo_sub, n[lt], s[lt])
            bm[p, lt] = closed(sroll(where(lo_sub, s[lt], n[lt]), 4))
        v = ends(n, s)
        bx[p, 2], bx[p, 3] = strip(l, X, v[0], v[1], e1, w1)
        m_e, m_w = strip(l, M, sroll(v[0], 4), sroll(v[1], 4), lroll(e1, 4), lroll(w1, 124))
        bm[p, 2], bm[p, 3] = closed(m_e), closed(m_w)

    def place_second(l):
        p = l + 1
        n, s = [nb[l, k] for k in range(3)], [sb[l, k] for k in range(3)]
        e1, w1, e2, w2 = em[l, 0], wm[l, 0], em[l, 1], wm[l, 1]
        for lt in range(2):
            bg[p, lt] = where(lo_sub, n[lt], s[lt])
            h = sroll(where(lo_sub, s[lt], n[lt]), 4)
            bh[p, lt] = h
            ba[p, lt] = where(lo_sub, sroll(h, 5), sroll(h, 3))
        v = ends(n, s)
        bg[p, 2], bg[p, 3] = strip(l, G, v[0], v[1], lroll(e1, 8), lroll(w1, 4))
        h = [sroll(t, 4) for t in v]
        bh[p, 2], bh[p, 3] = strip(l, H, h[0], h[1], e2, w2)
        a = [where(lo_half, sroll(t, 3), sroll(t, 5)) for t in h]
        ba[p, 2], ba[p, 3] = strip(l, A, a[0], a[1], lroll(e2, 4), lroll(w2, 124))

    for i in range(NL):
        place_first(NL * lev + i)
        place_second(NL * lev + i)

    for k, ref in ((16, em), (17, wm), (18, na), (19, sa)):
        share(k, ref, NL * other, NL).wait_recv()
    for i in range(NL):
        place_first(NL * other + i)
    share(20, nb, 1 + 3 * other, 3).wait_recv()
    share(21, sb, 1 + 3 * other, 3).wait_recv()
    for i in range(NL - 1):
        place_second(1 + 3 * other + i)

    def rim_of(full, part, p):
        return [
            full[p, 0, top, :], part[p, 0], full[p, 0, bottom, :],
            full[p, 1, top, :], part[p, 1], full[p, 1, bottom, :],
            part[p, 2], part[p, 3],
        ]

    def rim_east(v):
        r = [lroll(t, 127) for t in v]
        return [where(lane == 127, r[k + 3], r[k]) for k in range(3)] + r[3:]

    def rim_west(v):
        r = [lroll(t, 1) for t in v]
        return r[:3] + [where(lane == 0, r[k], r[k + 3]) for k in range(3)] + r[6:]

    def rim_north(v):
        r = [sroll(t, 7) for t in v]
        inside = [r[k] if k % 3 == 2 else where(sub == 7, r[k + 1], r[k]) for k in range(6)]
        return inside + [where(sub == 7, lroll(t, 116), t) for t in r[6:]]

    def rim_south(v):
        r = [sroll(t, 1) for t in v]
        inside = [r[k] if k % 3 == 0 else where(sub == 0, r[k - 1], r[k]) for k in range(6)]
        return inside + [where(sub == 0, lroll(t, 12), t) for t in r[6:]]

    fresh = (1, 4, 6, 7)
    below = rim_of(me, bm, lev)
    for j in range(2 * NL):
        p = 1 + j + lev
        m = rim_of(me, bm, p)
        e, n = rim_east(m), rim_north(m)
        for q, k in enumerate(fresh):
            vx[p, q] = jnp.maximum(m[k] + e[k], 0.0)
            vz[p, q] = jnp.maximum(0.5 * (m[k] + below[k]), 0.0)
            vy[p, q] = jnp.maximum(m[k] + n[k], 0.0)
        for q, k in enumerate((0, 3)):
            vy[p, 4 + q] = jnp.maximum(m[k] + n[k], 0.0)
        below = m

    def rim(u, base, count, finish, last=False):
        before, here = u(base - 1), u(base)

        def face(p, lo, hi):
            w = rim_of(wz, vz, p)
            return [w[k] * (hi[k] - lo[k]) for k in range(8)]

        fz = face(base, before, here)
        for j in range(count):
            p = base + j
            after = u(p + 1)
            fz_up = face(p + 1, here, after)
            w = rim_of(wx, vx, p)
            e = rim_east(here)
            fx = [w[k] * (e[k] - here[k]) for k in range(8)]
            fw = rim_west(fx)
            w = [
                vy[p, 4], vy[p, 0], wy[p, 0, bottom, :], vy[p, 5], vy[p, 1], wy[p, 1, bottom, :],
                vy[p, 2], vy[p, 3],
            ]
            n = rim_north(here)
            fy = [w[k] * (n[k] - here[k]) for k in range(8)]
            fs = rim_south(fy)
            finish(p, [(fx[k] - fw[k]) + (fy[k] - fs[k]) + (fz_up[k] - fz[k]) for k in range(8)])
            here, fz = after, fz_up

    def tiles(ref):
        return lambda p: [ref[p, k] for k in range(8)]

    def rim1(p, total):
        g = rim_of(ge, bg, p)
        for k in range(8):
            kr[p, k] = g[k] + 0.5 * total[k]

    def rim2(p, total):
        h = rim_of(he, bh, p)
        for k in range(8):
            x1r[p, k] = h[k] + total[k]

    def rim3(p, total):
        a = rim_of(ae, ba, p)
        for k in range(8):
            k2r[p, k] = (x1r[p, k] + a[k]) + 0.5 * total[k]

    def rim4(p, total):
        for k in range(8):
            x2r[p, k] = x1r[p, k] + total[k]

    rim(lambda p: rim_of(xe, bx, p), 1 + lev, 7, rim1)
    rim(tiles(kr), 1 + 2 * lev, 6, rim2)
    rim(tiles(x1r), 1 + 3 * lev, 5, rim3)
    rim(tiles(k2r), own, 4, rim4)

    def merge(i, _):
        p = own + i
        edge = where(halo_w, x2r[p, 6], x2r[p, 7])
        for r in range(RT):
            sl = pl.ds(8 * r, 8)
            cols = lroll(edge, 128 - (12 * (r + 1) + 8))
            for lt in range(2):
                cs = pl.ds(128 * lt, 128)
                noise = ra[i, sl, cs] * rw[1, i, sl, cs]
                at = (lane < 4) if lt == 0 else (lane >= 124)
                v = where(at, cols + noise, out[i, sl, cs])
                if r == 0:
                    v = where(lo_sub & ~at, x2r[p, 3 * lt + 2] + noise, v)
                if r == RT - 1:
                    v = where(~lo_sub & ~at, x2r[p, 3 * lt] + noise, v)
                out[i, sl, cs] = v
        return 0

    lax.fori_loop(0, NL, merge, 0)

    for c in to_side + to_core + relays:
        c.wait_send()

    @pl.when(south_in)
    def _():
        for c in to_south:
            c.wait_send()

    @pl.when(north_in)
    def _():
        for c in to_north:
            c.wait_send()

    @pl.when(at_fold)
    def _():
        for half in to_fold:
            for c in half:
                c.wait_send()


def local(*args):
    def vm(*shape, dtype=f32):
        return pltpu.VMEM(shape, dtype)

    cells = (NL, ROWS, COLS)
    tile = (8, 128)
    planes = (10, 2, ROWS, 128)
    rim = (2 * NL, 3) + tile
    sides = (2 * NL, 2) + tile
    rows = (NL, 2) + tile
    return pl.pallas_call(
        kernel,
        out_shape=pltpu.VMEM(cells, f32),
        in_specs=[pl.BlockSpec(memory_space=pltpu.HBM)] * 7,
        out_specs=pl.BlockSpec(memory_space=pltpu.VMEM),
        scratch_shapes=[
            vm(*cells), vm(*cells), vm(*cells), vm(*cells, dtype=jnp.int32), vm(2, *cells), vm(2, *cells),
            pltpu.SMEM((LON * COLS,), jnp.int32),
        ]
        + [vm(*planes)] * 11
        + [vm(NL, 2, ROWS, 128)] * 2
        + [vm(2 * NL, 5, 2, *tile)]
        + [vm(10, 4, *tile)] * 5
        + [vm(10, 4, *tile), vm(10, 6, *tile), vm(10, 4, *tile)]
        + [vm(10, 8, *tile)] * 4
        + [vm(*rim)] * 4
        + [vm(*sides)] * 2
        + [vm(*tile)] * 4
        + [vm(2 * LON, NL, *tile)] * 2
        + [vm(*rows)] * 4
        + [vm(*rows)] * 2
        + [vm(*tile)] * 2
        + [
            pltpu.SemaphoreType.DMA((7,)),
            pltpu.SemaphoreType.DMA((22,)),
            pltpu.SemaphoreType.DMA((22,)),
            pltpu.SemaphoreType.DMA((2, LON - 1)),
            pltpu.SemaphoreType.DMA((2, LON - 1)),
        ],
        compiler_params=pltpu.CompilerParams(
            collective_id=0, has_side_effects=True, vmem_limit_bytes=VMEM
        ),
        name="ocean",
    )(*(pltpu.with_memory_space_constraint(v, pltpu.HBM) for v in args))


def solution(mesh):
    block = P("lev", "lat", "lon")
    steps = P(None, "lev", "lat", "lon")
    return jax.shard_map(
        local,
        mesh=mesh,
        in_specs=(block, block, block, steps, steps, block, P()),
        out_specs=block,
        check_vma=False,
    )
```

time: 266 us -> 20.2 us (0.08)
  the two profiles are of different devices: /device:TPU:6 before, /device:TPU:229 now
where the time goes in v2:
time: 20.2 us; the launch traced here: 20.1 us
  Pallas kernels  19.4 us (96%)
  local copies, waits for them, and re-layouts  0.71 us (4%)
    pallas_call x1, Pallas kernels, local(): pl.pallas_call(kernel, out_shape=pltpu.VMEM(cells, f32), in_specs=[pl.Blo...  19.4 us
    unnamed x1, local copies, waits for them, and re-layouts  0.71 us

profile of v2, /device:TPU:229, one launch (start us, length us, event | category | flops | bytes accessed | tf_op | source)
XLA Modules:
  0.0 20.1 jit_solution(6679456147194117786)
XLA Ops:
  0.0 19.4 %ocean.1 = f32[4,64,256]{2,1,0:T(8,128)S(1)} custom-call(f32[4,64,256]{2,1,0:T(8,128)} %tracer.1, f32[4,64,256]{2,1,0:T(8,128)} %diff.1, f32[4,64,256]{2,1,0:T(8,128)} %amp.1, f32[2,4,64,256]{3,2,1,0:T(8,128)} %noise_w.1, f32[2,4,64,256]{3,2,1,0:T(8,128)} %noise_z.1, s32[4,64,256]{2,1,0:T(8,128)} %land.1, s32[2048]{0:T(1024)} %partner.1), custom_call_target="tpu_custom_call" | custom-call | tf_op jit(solution)/shard_map/ocean/pallas_call | solution.py:724
  19.4 0.7 %copy.9 = f32[4,64,256]{2,1,0:T(8,128)} copy(f32[4,64,256]{2,1,0:T(8,128)S(1)} %ocean.1) | data formatting | bytes 524288

commit v3 on v2

--- a/solution.py
+++ b/solution.py
@@ -18,8 +18,8 @@
 def kernel(
     tracer, diff, amp, noise_w, noise_z, land, partner, out,
     rx, rd, ra, rl, rw, rz, pc,
-    xe, me, ge, he, ae, ke, x1, k2, wx, wy, wz, mp, mr, so,
-    bx, bm, bg, bh, ba, vx, vy, vz, kr, x1r, k2r, x2r,
+    xe, me, ge, he, ae, ke, x1, k2, we, ww, wy, wz, mp, mr, so,
+    bx, bm, ve, vw, vn, vs, vz, kr, x1r, k2r, x2r, bg, bh, ba,
     na, sa, nb, sb, em, wm, dne, dnw, dse, dsw, fa, fb,
     tn1, ts1, tn2, ts2, ep, wp, dn, ds,
     isem, ssem, rsem, fsem_s, fsem_r,
@@ -53,7 +53,7 @@
 
     @pl.when(at_fold)
     def _():
-        for k in range(2, LON - 1):
+        for k in (2, 4, 6):
             greet(lon=lax.rem(lon + k, LON))
 
     greet(lev=other)
@@ -97,6 +97,24 @@
     def rows_at(r):
         return pl.ds(pl.multiple_of(8 * r, 8), 8)
 
+    for p in (0, 9):
+        for r in range(RT):
+            sl = pl.ds(8 * r, 8)
+            for lt in range(2):
+                me[p, lt, sl, :] = zero - 1.0
+                for ref in (xe, ke, x1, k2):
+                    ref[p, lt, sl, :] = zero
+            bm[p, sl, :] = zero - 1.0
+            for ref in (bx, kr, x1r, k2r):
+                ref[p, sl, :] = zero
+
+    @pl.when(lat == 0)
+    def _():
+        for i in range(NL):
+            for lt in range(3):
+                sa[NL * lev + i, lt] = zero
+                sb[NL * lev + i, lt] = zero
+
     for c in loads[:3]:
         c.wait()
 
@@ -150,11 +168,7 @@
     def _():
         pl.semaphore_wait(bar, 6)
 
-    @pl.when(at_fold)
-    def _():
-        pl.semaphore_wait(bar, 6 + LON - 3)
-
-    @pl.when(north_in & south_in)
+    @pl.when(south_in)
     def _():
         pl.semaphore_wait(bar, 9)
 
@@ -183,18 +197,28 @@
         send(8, ep, em.at[mine], lon=west),
         send(9, wp, wm.at[mine], lon=east),
     ]
-    block = pl.ds(2 * lon, 2)
-
-    def fold_copy(ref, slot, half, k):
+
+    def beside(i):
+        return i + 1 - 2 * lax.rem(i, 2)
+
+    def fold_copy(ref, half, n, owner, target):
+        slot = ref.at[pl.ds(2 * owner, 2)]
         return pltpu.make_async_remote_copy(
-            src_ref=ref.at[slot], dst_ref=ref.at[slot],
-            send_sem=fsem_s.at[half, k - 1], recv_sem=fsem_r.at[half, k - 1],
-            device_id={"lon": lax.rem(lon + k, LON)}, device_id_type=MESH,
+            src_ref=slot, dst_ref=slot, send_sem=fsem_s.at[half, n], recv_sem=fsem_r.at[half, n],
+            device_id={"lon": target}, device_id_type=MESH,
         )
 
-    to_fold = [
-        [fold_copy(ref, block, half, k) for k in range(1, LON)] for half, ref in enumerate((fa, fb))
-    ]
+    def fold_out(ref, half, n):
+        k = n if n < 4 else n - 3
+        target = beside(lon) if n == 0 else lax.rem(lon + 2 * k, LON)
+        return fold_copy(ref, half, n, lon if n < 4 else beside(lon), target)
+
+    def fold_in(ref, half, n):
+        k = n if n < 4 else n - 3
+        sender = beside(lon) if n == 0 else lax.rem(lon + LON - 2 * k, LON)
+        fold_copy(ref, half, n, sender if n < 4 else beside(sender), sender).wait_recv()
+
+    to_fold = [[fold_out(ref, half, n) for n in range(7)] for half, ref in enumerate((fa, fb))]
 
     def planes(ref, start, count):
         return ref.at[pl.ds(start, count)]
@@ -213,7 +237,7 @@
 
     @pl.when(at_fold)
     def _():
-        for c in to_fold[0]:
+        for c in to_fold[0][:4]:
             c.start()
 
     to_core = [share(10, xe, own, NL), send(11, mp, mr, lev=other)]
@@ -237,6 +261,10 @@
         return 0
 
     lax.fori_loop(0, NL, prep_second, 0)
+    late = [share(12, ge, 2 + 3 * lev, 3), share(13, he, 3 + 2 * lev, 2), share(14, ae, 4 + lev, 1)]
+    for c in late:
+        c.start()
+    to_core += late
 
     for i in range(NL):
         p = own + i
@@ -262,7 +290,7 @@
 
     @pl.when(at_fold)
     def _():
-        for c in to_fold[1]:
+        for c in to_fold[1][:4]:
             c.start()
 
     for halves, dst in (((tn1, tn2), dn), ((ts1, ts2), ds)):
@@ -307,148 +335,136 @@
     for c in to_side:
         c.start()
 
-    late = [
-        share(12, ge, 2 + 3 * lev, 3),
-        share(13, he, 3 + 2 * lev, 2),
-        share(14, ae, 4 + lev, 1),
-        share(15, so, NL * lev, NL),
-    ]
-    for c in late:
-        c.start()
-    to_core += late
-
-    for p in (0, 9):
-        for lt in range(2):
-            for r in range(RT):
-                sl = pl.ds(8 * r, 8)
-                me[p, lt, sl, :] = zero - 1.0
-                for ref in (xe, ke, x1, k2):
-                    ref[p, lt, sl, :] = zero
-        for k in range(4):
-            bx[p, k] = zero
-            bm[p, k] = zero - 1.0
-        for k in range(8):
-            for ref in (kr, x1r, k2r):
-                ref[p, k] = zero
-
-    @pl.when(lat == 0)
-    def _():
-        for i in range(NL):
-            for lt in range(3):
-                sa[NL * lev + i, lt] = zero
-                sb[NL * lev + i, lt] = zero
+    to_core.append(share(15, so, NL * lev, NL))
+    to_core[-1].start()
+
+    def pair(ref, p, r):
+        sl = pl.ds(8 * r, 8)
+        return [ref[p, lt, sl, :] for lt in range(2)]
+
+    def shifted(ref, p, r, d):
+        if 0 <= 8 * r + d <= ROWS - 8:
+            return [ref[p, lt, pl.ds(8 * r + d, 8), :] for lt in range(2)]
+        return [sroll(t, -d % 8) for t in pair(ref, p, r)]
+
+    def east_of(v):
+        r0, r1 = lroll(v[0], 127), lroll(v[1], 127)
+        return [where(lane == 127, r1, r0), r1]
+
+    def west_of(v):
+        r0, r1 = lroll(v[0], 1), lroll(v[1], 1)
+        return [r0, where(lane == 0, r0, r1)]
+
+    def relu(v):
+        return jnp.maximum(v, 0.0)
+
+    def weights(p, face):
+        for r in range(RT):
+            sl = pl.ds(8 * r, 8)
+            here, n = pair(me, p, r), shifted(me, p, r, 1)
+            e = east_of(here)
+            w = [relu(here[k] + e[k]) for k in range(2)]
+            v = west_of(w)
+            hi, lo = pair(me, face, r), pair(me, face - 1, r)
+            for k in range(2):
+                we[p, k, sl, :] = w[k]
+                ww[p, k, sl, :] = v[k]
+                wy[p, k, sl, :] = relu(here[k] + n[k])
+                wz[face, k, sl, :] = relu(0.5 * (hi[k] + lo[k]))
+
+    def inner(u, p, count, finish):
+        for r in range(RT):
+            stack = [pair(u, p + j, r) for j in range(-1, count + 1)]
+            fz = [
+                [w * (hi - lo) for w, lo, hi in zip(pair(wz, p + j, r), stack[j], stack[j + 1])]
+                for j in range(count + 1)
+            ]
+            for j in range(count):
+                here, q = stack[j + 1], p + j
+                n, s = shifted(u, q, r, 1), shifted(u, q, r, -1)
+                wn, ws = pair(wy, q, r), shifted(wy, q, r, -1)
+                e, w, v, wv = east_of(here), pair(we, q, r), west_of(here), pair(ww, q, r)
+                for k in range(2):
+                    total = (
+                        (w[k] * (e[k] - here[k]) - wv[k] * (here[k] - v[k]))
+                        + (wn[k] * (n[k] - here[k]) - ws[k] * (here[k] - s[k]))
+                        + (fz[j + 1][k] - fz[j][k])
+                    )
+                    finish(q, pl.ds(8 * r, 8), k, total)
+
+    def finish1(p, sl, k, total):
+        ke[p, k, sl, :] = ge[p, k, sl, :] + 0.5 * total
+
+    def finish2(p, sl, k, total):
+        x1[p, k, sl, :] = he[p, k, sl, :] + total
+
+    def finish3(p, sl, k, total):
+        k2[p, k, sl, :] = (x1[p, k, sl, :] + ae[p, k, sl, :]) + 0.5 * total
+
+    def finish4(p, sl, k, total):
+        j, cs = p - own, pl.ds(128 * k, 128)
+        out[j, sl, cs] = (x1[p, k, sl, :] + ra[j, sl, cs] * rw[1, j, sl, cs]) + total
+
+    far, near = 1 + 5 * lev, 4 - 2 * lev
+    next_own, next_faces = 2 + 3 * other, 5 - 3 * lev
+
+    def own_weights(j, _):
+        weights(own + j, far + j)
+        return 0
+
+    def other_weights(j, _):
+        weights(theirs + j, next_faces + j)
+        return 0
+
+    lax.fori_loop(0, NL, own_weights, 0)
+    inner(xe, far, 3, finish1)
+
+    def copy_own(i, _):
+        p = own + i
+        for ref, to in ((xe, bx), (me, bm)):
+            for lt in range(2):
+                to[p, pl.ds(24 * lt, 8), :] = ref[p, lt, top, :]
+                to[p, pl.ds(24 * lt + 16, 8), :] = ref[p, lt, bottom, :]
+        return 0
+
+    lax.fori_loop(0, NL, copy_own, 0)
+
+    @pl.when(at_fold)
+    def _():
+        for half, ref in enumerate((fa, fb)):
+            fold_in(ref, half, 0)
+            for c in to_fold[half][4:]:
+                c.start()
 
     share(10, xe, theirs, NL).wait_recv()
     to_core[1].wait_recv()
 
     def close(i, _):
+        p = theirs + i
         for r in range(RT):
             sl = pl.ds(8 * r, 8)
             for lt in range(2):
-                me[theirs + i, lt, sl, :] = closed(mr[i, lt, sl, :])
+                me[p, lt, sl, :] = closed(mr[i, lt, sl, :])
+        for ref, to in ((xe, bx), (me, bm)):
+            for lt in range(2):
+                to[p, pl.ds(24 * lt, 8), :] = ref[p, lt, top, :]
+                to[p, pl.ds(24 * lt + 16, 8), :] = ref[p, lt, bottom, :]
         return 0
 
     lax.fori_loop(0, NL, close, 0)
-
-    def pair(ref, p, r):
-        sl = pl.ds(8 * r, 8)
-        return [ref[p, lt, sl, :] for lt in range(2)]
-
-    def east_of(v):
-        r0, r1 = lroll(v[0], 127), lroll(v[1], 127)
-        return [where(lane == 127, r1, r0), r1]
-
-    def west_of(v):
-        r0, r1 = lroll(v[0], 1), lroll(v[1], 1)
-        return [r0, where(lane == 0, r0, r1)]
-
-    def weights(j, _):
-        p = j + lev + 1
-        nxt = [sroll(t, 7) for t in pair(me, p, 0)]
-        for r in range(RT):
-            sl = pl.ds(8 * r, 8)
-            here, here_up = pair(me, p, r), nxt
-            if r + 1 < RT:
-                nxt = [sroll(t, 7) for t in pair(me, p, r + 1)]
-            e = east_of(here)
-            below = pair(me, p - 1, r)
-            for lt in range(2):
-                n = where(sub == 7, nxt[lt], here_up[lt])
-                wx[p, lt, sl, :] = jnp.maximum(here[lt] + e[lt], 0.0)
-                wy[p, lt, sl, :] = jnp.maximum(here[lt] + n, 0.0)
-                wz[p, lt, sl, :] = jnp.maximum(0.5 * (here[lt] + below[lt]), 0.0)
+    lax.fori_loop(0, NL, other_weights, 0)
+    share(12, ge, next_own, 3).wait_recv()
+    inner(xe, near, 4, finish1)
+    share(13, he, 3 + 2 * other, 2).wait_recv()
+
+    def inner2(j, _):
+        inner(ke, 1 + 2 * lev + 3 * j, 3, finish2)
         return 0
 
-    lax.fori_loop(0, 2 * NL, weights, 0)
-
-    def inner(u, p, finish):
-        up_here = [sroll(t, 7) for t in pair(u, p, 0)]
-        before = [zero, zero]
-        for r in range(RT):
-            up_next = [sroll(t, 7) for t in pair(u, p, r + 1)] if r + 1 < RT else up_here
-            here = pair(u, p, r)
-            w = pair(wy, p, r)
-            fy = [w[k] * (where(sub == 7, up_next[k], up_here[k]) - here[k]) for k in range(2)]
-            fy_up = [sroll(t, 1) for t in fy]
-            e, w = east_of(here), pair(wx, p, r)
-            fx = [w[k] * (e[k] - here[k]) for k in range(2)]
-            fw = west_of(fx)
-            above, below = pair(u, p + 1, r), pair(u, p - 1, r)
-            wa, wb = pair(wz, p + 1, r), pair(wz, p, r)
-            for k in range(2):
-                fs = where(sub == 0, before[k], fy_up[k])
-                total = (
-                    (fx[k] - fw[k])
-                    + (fy[k] - fs)
-                    + (wa[k] * (above[k] - here[k]) - wb[k] * (here[k] - below[k]))
-                )
-                finish(pl.ds(8 * r, 8), k, total)
-            before, up_here = fy_up, up_next
-
-    def inner1(j, _):
-        p = 1 + j + lev
-
-        def finish(sl, k, total):
-            ke[p, k, sl, :] = ge[p, k, sl, :] + 0.5 * total
-
-        inner(xe, p, finish)
-        return 0
-
-    def inner2(j, _):
-        p = 1 + j + 2 * lev
-
-        def finish(sl, k, total):
-            x1[p, k, sl, :] = he[p, k, sl, :] + total
-
-        inner(ke, p, finish)
-        return 0
-
-    def inner3(j, _):
-        p = 1 + j + 3 * lev
-
-        def finish(sl, k, total):
-            k2[p, k, sl, :] = (x1[p, k, sl, :] + ae[p, k, sl, :]) + 0.5 * total
-
-        inner(x1, p, finish)
-        return 0
-
-    def inner4(j, _):
-        p = own + j
-
-        def finish(sl, k, total):
-            cs = pl.ds(128 * k, 128)
-            out[j, sl, cs] = (x1[p, k, sl, :] + ra[j, sl, cs] * rw[1, j, sl, cs]) + total
-
-        inner(k2, p, finish)
-        return 0
-
-    share(12, ge, 2 + 3 * other, 3).wait_recv()
-    lax.fori_loop(0, 7, inner1, 0)
-    share(13, he, 3 + 2 * other, 2).wait_recv()
-    lax.fori_loop(0, 6, inner2, 0)
+    lax.fori_loop(0, 2, inner2, 0)
     share(14, ae, 4 + other, 1).wait_recv()
-    lax.fori_loop(0, 5, inner3, 0)
-    lax.fori_loop(0, 4, inner4, 0)
+    inner(x1, 1 + 3 * lev, 5, finish3)
+    inner(k2, own, 4, finish4)
     share(15, so, NL * other, NL).wait_recv()
 
     relays = [
@@ -493,9 +509,8 @@
             dst[NL * lev + i, 2] = lroll(where(lo_half, v[0], v[3]), 116)
 
     def fold_arrived(ref, half):
-        for k in range(1, LON):
-            slot = pl.ds(2 * lax.rem(lon + LON - k, LON), 2)
-            fold_copy(ref, slot, half, k).wait_recv()
+        for n in range(1, 7):
+            fold_in(ref, half, n)
 
     @pl.when(north_in)
     def _():
@@ -519,13 +534,7 @@
     @pl.when(north_in)
     def _():
         to_south[1].wait_recv()
-
-    @pl.when(at_fold)
-    def _():
-        fold_arrived(fb, 1)
-        unfold(fb, nb)
-
-    relays[4].start()
+        relays[4].start()
 
     def ends(n, s):
         r = where(lo_half, lroll(both(s), 8), lroll(both(n), 116))
@@ -538,46 +547,42 @@
             where(ring_w, v_w, where(halo_w, from_w, so[l, f, 1])),
         )
 
+    def put(ref, p, tiles, which):
+        for k, t in zip(which, tiles):
+            ref[p, pl.ds(8 * k, 8), :] = t
+
+    fresh = (1, 4, 6, 7)
+
     def place_first(l):
         p = l + 1
         n, s = [na[l, k] for k in range(3)], [sa[l, k] for k in range(3)]
         e1, w1 = em[l, 0], wm[l, 0]
-        for lt in range(2):
-            bx[p, lt] = where(lo_sub, n[lt], s[lt])
-            bm[p, lt] = closed(sroll(where(lo_sub, s[lt], n[lt]), 4))
         v = ends(n, s)
-        bx[p, 2], bx[p, 3] = strip(l, X, v[0], v[1], e1, w1)
-        m_e, m_w = strip(l, M, sroll(v[0], 4), sroll(v[1], 4), lroll(e1, 4), lroll(w1, 124))
-        bm[p, 2], bm[p, 3] = closed(m_e), closed(m_w)
+        x = [where(lo_sub, n[lt], s[lt]) for lt in range(2)]
+        m = [sroll(where(lo_sub, s[lt], n[lt]), 4) for lt in range(2)]
+        x += strip(l, X, v[0], v[1], e1, w1)
+        m += strip(l, M, sroll(v[0], 4), sroll(v[1], 4), lroll(e1, 4), lroll(w1, 124))
+        put(bx, p, x, fresh)
+        put(bm, p, [closed(t) for t in m], fresh)
 
     def place_second(l):
         p = l + 1
         n, s = [nb[l, k] for k in range(3)], [sb[l, k] for k in range(3)]
         e1, w1, e2, w2 = em[l, 0], wm[l, 0], em[l, 1], wm[l, 1]
-        for lt in range(2):
-            bg[p, lt] = where(lo_sub, n[lt], s[lt])
-            h = sroll(where(lo_sub, s[lt], n[lt]), 4)
-            bh[p, lt] = h
-            ba[p, lt] = where(lo_sub, sroll(h, 5), sroll(h, 3))
         v = ends(n, s)
-        bg[p, 2], bg[p, 3] = strip(l, G, v[0], v[1], lroll(e1, 8), lroll(w1, 4))
-        h = [sroll(t, 4) for t in v]
-        bh[p, 2], bh[p, 3] = strip(l, H, h[0], h[1], e2, w2)
-        a = [where(lo_half, sroll(t, 3), sroll(t, 5)) for t in h]
-        ba[p, 2], ba[p, 3] = strip(l, A, a[0], a[1], lroll(e2, 4), lroll(w2, 124))
-
-    for i in range(NL):
-        place_first(NL * lev + i)
-        place_second(NL * lev + i)
-
-    for k, ref in ((16, em), (17, wm), (18, na), (19, sa)):
-        share(k, ref, NL * other, NL).wait_recv()
-    for i in range(NL):
-        place_first(NL * other + i)
-    share(20, nb, 1 + 3 * other, 3).wait_recv()
-    share(21, sb, 1 + 3 * other, 3).wait_recv()
-    for i in range(NL - 1):
-        place_second(1 + 3 * other + i)
+        g = [where(lo_sub, n[lt], s[lt]) for lt in range(2)]
+        h = [sroll(where(lo_sub, s[lt], n[lt]), 4) for lt in range(2)]
+        a = [where(lo_sub, sroll(t, 5), sroll(t, 3)) for t in h]
+        g += strip(l, G, v[0], v[1], lroll(e1, 8), lroll(w1, 4))
+        hs = [sroll(t, 4) for t in v]
+        h += strip(l, H, hs[0], hs[1], e2, w2)
+        a_s = [where(lo_half, sroll(t, 3), sroll(t, 5)) for t in hs]
+        a += strip(l, A, a_s[0], a_s[1], lroll(e2, 4), lroll(w2, 124))
+        for k in range(4):
+            bg[p, k], bh[p, k], ba[p, k] = g[k], h[k], a[k]
+
+    def tiles(ref, p):
+        return [ref[p, pl.ds(8 * k, 8), :] for k in range(8)]
 
     def rim_of(full, part, p):
         return [
@@ -594,86 +599,124 @@
         r = [lroll(t, 1) for t in v]
         return r[:3] + [where(lane == 0, r[k], r[k + 3]) for k in range(3)] + r[6:]
 
-    def rim_north(v):
-        r = [sroll(t, 7) for t in v]
-        inside = [r[k] if k % 3 == 2 else where(sub == 7, r[k + 1], r[k]) for k in range(6)]
-        return inside + [where(sub == 7, lroll(t, 116), t) for t in r[6:]]
-
-    def rim_south(v):
-        r = [sroll(t, 1) for t in v]
-        inside = [r[k] if k % 3 == 0 else where(sub == 0, r[k - 1], r[k]) for k in range(6)]
-        return inside + [where(sub == 0, lroll(t, 12), t) for t in r[6:]]
-
-    fresh = (1, 4, 6, 7)
-    below = rim_of(me, bm, lev)
-    for j in range(2 * NL):
-        p = 1 + j + lev
-        m = rim_of(me, bm, p)
-        e, n = rim_east(m), rim_north(m)
-        for q, k in enumerate(fresh):
-            vx[p, q] = jnp.maximum(m[k] + e[k], 0.0)
-            vz[p, q] = jnp.maximum(0.5 * (m[k] + below[k]), 0.0)
-            vy[p, q] = jnp.maximum(m[k] + n[k], 0.0)
-        for q, k in enumerate((0, 3)):
-            vy[p, 4 + q] = jnp.maximum(m[k] + n[k], 0.0)
-        below = m
-
-    def rim(u, base, count, finish, last=False):
-        before, here = u(base - 1), u(base)
-
-        def face(p, lo, hi):
-            w = rim_of(wz, vz, p)
-            return [w[k] * (hi[k] - lo[k]) for k in range(8)]
-
-        fz = face(base, before, here)
+    def strip_north(t):
+        r = sroll(t, 7)
+        return where(sub == 7, lroll(r, 116), r)
+
+    def strip_south(t):
+        r = sroll(t, 1)
+        return where(sub == 0, lroll(r, 12), r)
+
+    def rim_north(ref, p, v):
+        inside = [sroll(v[k], 7) if k % 3 == 2 else ref[p, pl.ds(8 * k + 1, 8), :] for k in range(6)]
+        return inside + [strip_north(t) for t in v[6:]]
+
+    def rim_south(ref, p, v):
+        inside = [sroll(v[k], 1) if k % 3 == 0 else ref[p, pl.ds(8 * k - 1, 8), :] for k in range(6)]
+        return inside + [strip_south(t) for t in v[6:]]
+
+    every = range(8)
+
+    def rim_weights(p):
+        m = tiles(bm, p)
+        e, n = rim_east(m), rim_north(bm, p, m)
+        w = [relu(m[k] + e[k]) for k in every]
+        y = [relu(m[k] + n[k]) for k in every]
+        put(ve, p, w, every)
+        put(vw, p, rim_west(w), every)
+        put(vn, p, y, every)
+        put(vs, p, rim_south(vn, p, y), every)
+
+    def rim_faces(p):
+        lo, hi = tiles(bm, p - 1), tiles(bm, p)
+        put(vz, p, [relu(0.5 * (hi[k] + lo[k])) for k in every], every)
+
+    def rim(u, base, count, finish):
+        stack = [tiles(u, base + j) for j in range(-1, count + 1)]
+
+        def face(j):
+            w = tiles(vz, base + j)
+            return [w[k] * (stack[j + 1][k] - stack[j][k]) for k in every]
+
+        fz = face(0)
         for j in range(count):
-            p = base + j
-            after = u(p + 1)
-            fz_up = face(p + 1, here, after)
-            w = rim_of(wx, vx, p)
-            e = rim_east(here)
-            fx = [w[k] * (e[k] - here[k]) for k in range(8)]
-            fw = rim_west(fx)
-            w = [
-                vy[p, 4], vy[p, 0], wy[p, 0, bottom, :], vy[p, 5], vy[p, 1], wy[p, 1, bottom, :],
-                vy[p, 2], vy[p, 3],
-            ]
-            n = rim_north(here)
-            fy = [w[k] * (n[k] - here[k]) for k in range(8)]
-            fs = rim_south(fy)
-            finish(p, [(fx[k] - fw[k]) + (fy[k] - fs[k]) + (fz_up[k] - fz[k]) for k in range(8)])
-            here, fz = after, fz_up
-
-    def tiles(ref):
-        return lambda p: [ref[p, k] for k in range(8)]
+            p, here = base + j, stack[j + 1]
+            fz_up = face(j + 1)
+            e, w, n, s = rim_east(here), rim_west(here), rim_north(u, p, here), rim_south(u, p, here)
+            we_, ww_, wn_, ws_ = (tiles(ref, p) for ref in (ve, vw, vn, vs))
+            finish(
+                p,
+                [
+                    (we_[k] * (e[k] - here[k]) - ww_[k] * (here[k] - w[k]))
+                    + (wn_[k] * (n[k] - here[k]) - ws_[k] * (here[k] - s[k]))
+                    + (fz_up[k] - fz[k])
+                    for k in every
+                ],
+            )
+            fz = fz_up
 
     def rim1(p, total):
-        g = rim_of(ge, bg, p)
-        for k in range(8):
-            kr[p, k] = g[k] + 0.5 * total[k]
+        put(kr, p, [0.5 * t for t in total], every)
 
     def rim2(p, total):
         h = rim_of(he, bh, p)
-        for k in range(8):
-            x1r[p, k] = h[k] + total[k]
+        put(x1r, p, [h[k] + total[k] for k in every], every)
 
     def rim3(p, total):
-        a = rim_of(ae, ba, p)
-        for k in range(8):
-            k2r[p, k] = (x1r[p, k] + a[k]) + 0.5 * total[k]
+        a, x = rim_of(ae, ba, p), tiles(x1r, p)
+        put(k2r, p, [(x[k] + a[k]) + 0.5 * total[k] for k in every], every)
 
     def rim4(p, total):
-        for k in range(8):
-            x2r[p, k] = x1r[p, k] + total[k]
-
-    rim(lambda p: rim_of(xe, bx, p), 1 + lev, 7, rim1)
-    rim(tiles(kr), 1 + 2 * lev, 6, rim2)
-    rim(tiles(x1r), 1 + 3 * lev, 5, rim3)
-    rim(tiles(k2r), own, 4, rim4)
+        x = tiles(x1r, p)
+        put(x2r, p, [x[k] + total[k] for k in every], every)
+
+    def add_noise(p):
+        g, k_ = rim_of(ge, bg, p), tiles(kr, p)
+        put(kr, p, [g[k] + k_[k] for k in every], every)
+
+    for i in range(NL):
+        place_first(NL * lev + i)
+    for i in range(NL):
+        rim_weights(own + i)
+    for i in range(NL):
+        rim_faces(far + i)
+    rim(bx, far, 3, rim1)
+
+    for k, ref in ((16, em), (17, wm), (18, na), (19, sa)):
+        share(k, ref, NL * other, NL).wait_recv()
+    for i in range(NL):
+        place_first(NL * other + i)
+    for i in range(3):
+        rim_weights(next_own + i)
+    for i in range(NL):
+        rim_faces(next_faces + i)
+    rim(bx, near, 4, rim1)
+
+    @pl.when(at_fold)
+    def _():
+        fold_arrived(fb, 1)
+        unfold(fb, nb)
+        relays[4].start()
+
+    for i in range(NL):
+        place_second(NL * lev + i)
+    for i in range(NL):
+        add_noise(own + i)
+    rim(kr, far, 3, rim2)
+    share(20, nb, 1 + 3 * other, 3).wait_recv()
+    share(21, sb, 1 + 3 * other, 3).wait_recv()
+    for i in range(NL - 1):
+        place_second(1 + 3 * other + i)
+    for i in range(NL - 1):
+        add_noise(next_own + i)
+    rim(kr, 4 - lev, 3, rim2)
+    rim(x1r, 1 + 3 * lev, 5, rim3)
+    rim(k2r, own, 4, rim4)
 
     def merge(i, _):
         p = own + i
-        edge = where(halo_w, x2r[p, 6], x2r[p, 7])
+        t = tiles(x2r, p)
+        edge = where(halo_w, t[6], t[7])
         for r in range(RT):
             sl = pl.ds(8 * r, 8)
             cols = lroll(edge, 128 - (12 * (r + 1) + 8))
@@ -683,9 +726,9 @@
                 at = (lane < 4) if lt == 0 else (lane >= 124)
                 v = where(at, cols + noise, out[i, sl, cs])
                 if r == 0:
-                    v = where(lo_sub & ~at, x2r[p, 3 * lt + 2] + noise, v)
+                    v = where(lo_sub & ~at, t[3 * lt + 2] + noise, v)
                 if r == RT - 1:
-                    v = where(~lo_sub & ~at, x2r[p, 3 * lt] + noise, v)
+                    v = where(~lo_sub & ~at, t[3 * lt] + noise, v)
                 out[i, sl, cs] = v
         return 0
 
@@ -730,12 +773,11 @@
             vm(*cells), vm(*cells), vm(*cells), vm(*cells, dtype=jnp.int32), vm(2, *cells), vm(2, *cells),
             pltpu.SMEM((LON * COLS,), jnp.int32),
         ]
-        + [vm(*planes)] * 11
+        + [vm(*planes)] * 12
         + [vm(NL, 2, ROWS, 128)] * 2
         + [vm(2 * NL, 5, 2, *tile)]
-        + [vm(10, 4, *tile)] * 5
-        + [vm(10, 4, *tile), vm(10, 6, *tile), vm(10, 4, *tile)]
-        + [vm(10, 8, *tile)] * 4
+        + [vm(10, 64, 128)] * 11
+        + [vm(10, 4, *tile)] * 3
         + [vm(*rim)] * 4
         + [vm(*sides)] * 2
         + [vm(*tile)] * 4

time: 20.2 us -> 18 us (0.89)
  the two profiles are of different devices: /device:TPU:229 before, /device:TPU:5 now
where the time goes in v3:
time: 18 us; the launch traced here: 17.9 us
  Pallas kernels  17.2 us (96%)
  local copies, waits for them, and re-layouts  0.71 us (4%)
    pallas_call x1, Pallas kernels, local(): pl.pallas_call(kernel, out_shape=pltpu.VMEM(cells, f32), in_specs=[pl.Blo...  17.2 us
    unnamed x1, local copies, waits for them, and re-layouts  0.71 us

profile of v3, /device:TPU:5, one launch (start us, length us, event | category | flops | bytes accessed | tf_op | source)
XLA Modules:
  0.0 17.9 jit_solution(2271078794167425879)
XLA Ops:
  0.0 17.2 %ocean.1 = f32[4,64,256]{2,1,0:T(8,128)S(1)} custom-call(f32[4,64,256]{2,1,0:T(8,128)} %tracer.1, f32[4,64,256]{2,1,0:T(8,128)} %diff.1, f32[4,64,256]{2,1,0:T(8,128)} %amp.1, f32[2,4,64,256]{3,2,1,0:T(8,128)} %noise_w.1, f32[2,4,64,256]{3,2,1,0:T(8,128)} %noise_z.1, s32[4,64,256]{2,1,0:T(8,128)} %land.1, s32[2048]{0:T(1024)} %partner.1), custom_call_target="tpu_custom_call" | custom-call | tf_op jit(solution)/shard_map/ocean/pallas_call | solution.py:767
  17.2 0.7 %copy.9 = f32[4,64,256]{2,1,0:T(8,128)} copy(f32[4,64,256]{2,1,0:T(8,128)S(1)} %ocean.1) | data formatting | bytes 524288

commit v4 on v3

--- a/solution.py
+++ b/solution.py
@@ -18,8 +18,8 @@
 def kernel(
     tracer, diff, amp, noise_w, noise_z, land, partner, out,
     rx, rd, ra, rl, rw, rz, pc,
-    xe, me, ge, he, ae, ke, x1, k2, we, ww, wy, wz, mp, mr, so,
-    bx, bm, ve, vw, vn, vs, vz, kr, x1r, k2r, x2r, bg, bh, ba,
+    xe, me, ge, he, ae, ke, x1, k2, we, ww, wy, wz, mp, mr, qe, so,
+    bx, bm, vn, vs, kr, x1r, k2r, x2r, bg, bh, ba, ve, vw, vz,
     na, sa, nb, sb, em, wm, dne, dnw, dse, dsw, fa, fb,
     tn1, ts1, tn2, ts2, ep, wp, dn, ds,
     isem, ssem, rsem, fsem_s, fsem_r,
@@ -163,6 +163,79 @@
             for lt in range(2):
                 x, m = mirror_rows(xe[own + i, lt, top, :]), mirror_rows(mp[i, lt, top, :])
                 fa[2 * lon + lt, i] = mirror_lanes(first_rows(x, m))
+
+    def pack_strip(i, f, ref, q):
+        s_e, s_w = zero, zero
+        for r in range(RT):
+            sl = pl.ds(8 * r, 8)
+            v = lroll(where(lo_half, ref[q, 0, sl, :], ref[q, 1, sl, :]), 12 * (r + 1) + 8)
+            s_e = where(group_e == r + 1, v, s_e)
+            s_w = where(group_w == r + 1, v, s_w)
+        so[own + i - 1, f, 0] = s_e
+        so[own + i - 1, f, 1] = s_w
+
+    def strips_first(i, _):
+        pack_strip(i, X, xe, own + i)
+        pack_strip(i, M, mp, i)
+        return 0
+
+    lax.fori_loop(0, NL, strips_first, 0)
+
+    for c in loads[3:]:
+        c.wait()
+
+    def prep_second(i, _):
+        p = own + i
+        for r in range(RT):
+            sl = pl.ds(8 * r, 8)
+            for lt in range(2):
+                cs = pl.ds(128 * lt, 128)
+                x = rx[i, sl, cs]
+                amp_ = ra[i, sl, cs]
+                ge[p, lt, sl, :] = x + amp_ * rz[0, i, sl, cs]
+                he[p, lt, sl, :] = x + amp_ * rw[0, i, sl, cs]
+                ae[p, lt, sl, :] = amp_ * rz[1, i, sl, cs]
+                qe[i, lt, sl, :] = amp_ * rw[1, i, sl, cs]
+        return 0
+
+    lax.fori_loop(0, NL, prep_second, 0)
+    for i in range(NL):
+        p = own + i
+        for lt in range(2):
+            tn2[i, lt] = first_rows2(ge[p, lt, bottom, :], he[p, lt, bottom, :], ae[p, lt, bottom, :])
+            ts2[i, lt] = last_rows2(ge[p, lt, top, :], he[p, lt, top, :], ae[p, lt, top, :])
+
+    @pl.when(at_fold)
+    def _():
+        for i in range(NL):
+            p = own + i
+            for lt in range(2):
+                g, h, a = (mirror_rows(ref[p, lt, top, :]) for ref in (ge, he, ae))
+                fb[2 * lon + lt, i] = mirror_lanes(first_rows2(g, h, a))
+
+    for halves, dst in (((tn1, tn2), dn), ((ts1, ts2), ds)):
+        d = zero
+        for i in range(NL):
+            for n, half in enumerate(halves):
+                k = 2 * i + n
+                d = where((lane >> 3) == k, lroll(both(half[i]), 8 * k + 4), d)
+        dst[...] = d
+
+    def strips_second(i, _):
+        for f, ref in ((G, ge), (H, he), (A, ae)):
+            pack_strip(i, f, ref, own + i)
+        x, m, g, h, a = (so[own + i - 1, f, 0] for f in range(5))
+        ep[i, 0] = where(halo_e, x, where(halo_w, lroll(m, 124), lroll(g, 120)))
+        ep[i, 1] = where(halo_e, h, lroll(a, 124))
+        wp[i, 0] = where(halo_w, x, where(halo_e, lroll(m, 4), lroll(g, 124)))
+        wp[i, 1] = where(halo_w, h, lroll(a, 4))
+        return 0
+
+    early = lax.rem(lat, LAT // 2) < LAT // 4
+
+    @pl.when(early)
+    def _():
+        lax.fori_loop(0, NL, strips_second, 0)
 
     @pl.when(lat == 0)
     def _():
@@ -227,116 +300,45 @@
         part = planes(ref, start, count)
         return send(k, part, part, lev=other)
 
+    @pl.when(at_fold)
+    def _():
+        for half in to_fold:
+            for c in half[:4]:
+                c.start()
+
     @pl.when(south_in)
     def _():
-        to_south[0].start()
+        for k in (2, 3, 0, 1):
+            to_south[k].start()
 
     @pl.when(north_in)
     def _():
-        to_north[0].start()
-
-    @pl.when(at_fold)
-    def _():
-        for c in to_fold[0][:4]:
+        for k in (2, 3, 0, 1):
+            to_north[k].start()
+
+    @pl.when(early)
+    def _():
+        for c in to_side:
             c.start()
 
-    to_core = [share(10, xe, own, NL), send(11, mp, mr, lev=other)]
-    for c in to_core:
+    to_core = [
+        share(10, xe, own, NL),
+        send(11, mp, mr, lev=other),
+        share(12, ge, 2 + 3 * lev, 3),
+        share(13, he, 3 + 2 * lev, 2),
+        share(14, ae, 4 + lev, 1),
+        share(15, so, NL * lev, NL),
+    ]
+    for c in to_core[:5]:
         c.start()
 
-    for c in loads[3:]:
-        c.wait()
-
-    def prep_second(i, _):
-        p = own + i
-        for r in range(RT):
-            sl = pl.ds(8 * r, 8)
-            for lt in range(2):
-                cs = pl.ds(128 * lt, 128)
-                x = rx[i, sl, cs]
-                amp_ = ra[i, sl, cs]
-                ge[p, lt, sl, :] = x + amp_ * rz[0, i, sl, cs]
-                he[p, lt, sl, :] = x + amp_ * rw[0, i, sl, cs]
-                ae[p, lt, sl, :] = amp_ * rz[1, i, sl, cs]
-        return 0
-
-    lax.fori_loop(0, NL, prep_second, 0)
-    late = [share(12, ge, 2 + 3 * lev, 3), share(13, he, 3 + 2 * lev, 2), share(14, ae, 4 + lev, 1)]
-    for c in late:
-        c.start()
-    to_core += late
-
-    for i in range(NL):
-        p = own + i
-        for lt in range(2):
-            tn2[i, lt] = first_rows2(ge[p, lt, bottom, :], he[p, lt, bottom, :], ae[p, lt, bottom, :])
-            ts2[i, lt] = last_rows2(ge[p, lt, top, :], he[p, lt, top, :], ae[p, lt, top, :])
-
-    @pl.when(at_fold)
-    def _():
-        for i in range(NL):
-            p = own + i
-            for lt in range(2):
-                g, h, a = (mirror_rows(ref[p, lt, top, :]) for ref in (ge, he, ae))
-                fb[2 * lon + lt, i] = mirror_lanes(first_rows2(g, h, a))
-
-    @pl.when(south_in)
-    def _():
-        to_south[1].start()
-
-    @pl.when(north_in)
-    def _():
-        to_north[1].start()
-
-    @pl.when(at_fold)
-    def _():
-        for c in to_fold[1][:4]:
+    @pl.when(jnp.logical_not(early))
+    def _():
+        lax.fori_loop(0, NL, strips_second, 0)
+        for c in to_side:
             c.start()
 
-    for halves, dst in (((tn1, tn2), dn), ((ts1, ts2), ds)):
-        d = zero
-        for i in range(NL):
-            for n, half in enumerate(halves):
-                k = 2 * i + n
-                d = where((lane >> 3) == k, lroll(both(half[i]), 8 * k + 4), d)
-        dst[...] = d
-
-    @pl.when(south_in)
-    def _():
-        to_south[2].start()
-        to_south[3].start()
-
-    @pl.when(north_in)
-    def _():
-        to_north[2].start()
-        to_north[3].start()
-
-    def pack_strips(i, _):
-        p = own + i
-        strips = []
-        for f, ref, q in ((X, xe, p), (M, mp, i), (G, ge, p), (H, he, p), (A, ae, p)):
-            s_e, s_w = zero, zero
-            for r in range(RT):
-                sl = pl.ds(8 * r, 8)
-                v = lroll(where(lo_half, ref[q, 0, sl, :], ref[q, 1, sl, :]), 12 * (r + 1) + 8)
-                s_e = where(group_e == r + 1, v, s_e)
-                s_w = where(group_w == r + 1, v, s_w)
-            so[p - 1, f, 0] = s_e
-            so[p - 1, f, 1] = s_w
-            strips.append(s_e)
-        x, m, g, h, a = strips
-        ep[i, 0] = where(halo_e, x, where(halo_w, lroll(m, 124), lroll(g, 120)))
-        ep[i, 1] = where(halo_e, h, lroll(a, 124))
-        wp[i, 0] = where(halo_w, x, where(halo_e, lroll(m, 4), lroll(g, 124)))
-        wp[i, 1] = where(halo_w, h, lroll(a, 4))
-        return 0
-
-    lax.fori_loop(0, NL, pack_strips, 0)
-    for c in to_side:
-        c.start()
-
-    to_core.append(share(15, so, NL * lev, NL))
-    to_core[-1].start()
+    to_core[5].start()
 
     def pair(ref, p, r):
         sl = pl.ds(8 * r, 8)
@@ -402,8 +404,8 @@
         k2[p, k, sl, :] = (x1[p, k, sl, :] + ae[p, k, sl, :]) + 0.5 * total
 
     def finish4(p, sl, k, total):
-        j, cs = p - own, pl.ds(128 * k, 128)
-        out[j, sl, cs] = (x1[p, k, sl, :] + ra[j, sl, cs] * rw[1, j, sl, cs]) + total
+        j = p - own
+        out[j, sl, pl.ds(128 * k, 128)] = (x1[p, k, sl, :] + qe[j, k, sl, :]) + total
 
     far, near = 1 + 5 * lev, 4 - 2 * lev
     next_own, next_faces = 2 + 3 * other, 5 - 3 * lev
@@ -466,6 +468,25 @@
     inner(x1, 1 + 3 * lev, 5, finish3)
     inner(k2, own, 4, finish4)
     share(15, so, NL * other, NL).wait_recv()
+
+    for c in to_side + to_core:
+        c.wait_send()
+
+    @pl.when(south_in)
+    def _():
+        for c in to_south:
+            c.wait_send()
+
+    @pl.when(north_in)
+    def _():
+        for c in to_north:
+            c.wait_send()
+
+    @pl.when(at_fold)
+    def _():
+        for half in to_fold:
+            for c in half:
+                c.wait_send()
 
     relays = [
         share(16, em, NL * lev, NL),
@@ -621,21 +642,23 @@
         m = tiles(bm, p)
         e, n = rim_east(m), rim_north(bm, p, m)
         w = [relu(m[k] + e[k]) for k in every]
+        v = rim_west(w)
+        for q, k in enumerate(fresh):
+            ve[p, q], vw[p, q] = w[k], v[k]
         y = [relu(m[k] + n[k]) for k in every]
-        put(ve, p, w, every)
-        put(vw, p, rim_west(w), every)
         put(vn, p, y, every)
         put(vs, p, rim_south(vn, p, y), every)
 
     def rim_faces(p):
-        lo, hi = tiles(bm, p - 1), tiles(bm, p)
-        put(vz, p, [relu(0.5 * (hi[k] + lo[k])) for k in every], every)
+        for q, k in enumerate(fresh):
+            sl = pl.ds(8 * k, 8)
+            vz[p, q] = relu(0.5 * (bm[p, sl, :] + bm[p - 1, sl, :]))
 
     def rim(u, base, count, finish):
         stack = [tiles(u, base + j) for j in range(-1, count + 1)]
 
         def face(j):
-            w = tiles(vz, base + j)
+            w = rim_of(wz, vz, base + j)
             return [w[k] * (stack[j + 1][k] - stack[j][k]) for k in every]
 
         fz = face(0)
@@ -643,7 +666,8 @@
             p, here = base + j, stack[j + 1]
             fz_up = face(j + 1)
             e, w, n, s = rim_east(here), rim_west(here), rim_north(u, p, here), rim_south(u, p, here)
-            we_, ww_, wn_, ws_ = (tiles(ref, p) for ref in (ve, vw, vn, vs))
+            we_, ww_ = rim_of(we, ve, p), rim_of(ww, vw, p)
+            wn_, ws_ = tiles(vn, p), tiles(vs, p)
             finish(
                 p,
                 [
@@ -682,6 +706,19 @@
         rim_faces(far + i)
     rim(bx, far, 3, rim1)
 
+    @pl.when(at_fold)
+    def _():
+        fold_arrived(fb, 1)
+        unfold(fb, nb)
+        relays[4].start()
+
+    for i in range(NL):
+        place_second(NL * lev + i)
+    for i in range(3):
+        add_noise(far + i)
+    rim(kr, 1 + 6 * lev, 2, rim2)
+    rim(x1r, 1 + 7 * lev, 1, rim3)
+
     for k, ref in ((16, em), (17, wm), (18, na), (19, sa)):
         share(k, ref, NL * other, NL).wait_recv()
     for i in range(NL):
@@ -691,67 +728,31 @@
     for i in range(NL):
         rim_faces(next_faces + i)
     rim(bx, near, 4, rim1)
-
-    @pl.when(at_fold)
-    def _():
-        fold_arrived(fb, 1)
-        unfold(fb, nb)
-        relays[4].start()
-
-    for i in range(NL):
-        place_second(NL * lev + i)
-    for i in range(NL):
-        add_noise(own + i)
-    rim(kr, far, 3, rim2)
     share(20, nb, 1 + 3 * other, 3).wait_recv()
     share(21, sb, 1 + 3 * other, 3).wait_recv()
     for i in range(NL - 1):
         place_second(1 + 3 * other + i)
-    for i in range(NL - 1):
-        add_noise(next_own + i)
-    rim(kr, 4 - lev, 3, rim2)
-    rim(x1r, 1 + 3 * lev, 5, rim3)
+    for i in range(NL):
+        add_noise(near + i)
+    rim(kr, 3, 4, rim2)
+    rim(x1r, 2 + 2 * lev, 4, rim3)
     rim(k2r, own, 4, rim4)
 
-    def merge(i, _):
-        p = own + i
-        t = tiles(x2r, p)
+    for i in range(NL):
+        t = tiles(x2r, own + i)
         edge = where(halo_w, t[6], t[7])
+        for lt in range(2):
+            cs = pl.ds(128 * lt, 128)
+            pltpu.store(out.at[i, bottom, cs], t[3 * lt + 2] + qe[i, lt, bottom, :], mask=lo_sub)
+            pltpu.store(out.at[i, top, cs], t[3 * lt] + qe[i, lt, top, :], mask=sub >= 4)
         for r in range(RT):
             sl = pl.ds(8 * r, 8)
             cols = lroll(edge, 128 - (12 * (r + 1) + 8))
-            for lt in range(2):
-                cs = pl.ds(128 * lt, 128)
-                noise = ra[i, sl, cs] * rw[1, i, sl, cs]
-                at = (lane < 4) if lt == 0 else (lane >= 124)
-                v = where(at, cols + noise, out[i, sl, cs])
-                if r == 0:
-                    v = where(lo_sub & ~at, t[3 * lt + 2] + noise, v)
-                if r == RT - 1:
-                    v = where(~lo_sub & ~at, t[3 * lt] + noise, v)
-                out[i, sl, cs] = v
-        return 0
-
-    lax.fori_loop(0, NL, merge, 0)
-
-    for c in to_side + to_core + relays:
+            pltpu.store(out.at[i, sl, pl.ds(0, 128)], cols + qe[i, 0, sl, :], mask=lane < 4)
+            pltpu.store(out.at[i, sl, pl.ds(128, 128)], cols + qe[i, 1, sl, :], mask=lane >= 124)
+
+    for c in relays:
         c.wait_send()
-
-    @pl.when(south_in)
-    def _():
-        for c in to_south:
-            c.wait_send()
-
-    @pl.when(north_in)
-    def _():
-        for c in to_north:
-            c.wait_send()
-
-    @pl.when(at_fold)
-    def _():
-        for half in to_fold:
-            for c in half:
-                c.wait_send()
 
 
 def local(*args):
@@ -774,10 +775,10 @@
             pltpu.SMEM((LON * COLS,), jnp.int32),
         ]
         + [vm(*planes)] * 12
-        + [vm(NL, 2, ROWS, 128)] * 2
+        + [vm(NL, 2, ROWS, 128)] * 3
         + [vm(2 * NL, 5, 2, *tile)]
-        + [vm(10, 64, 128)] * 11
-        + [vm(10, 4, *tile)] * 3
+        + [vm(10, 64, 128)] * 8
+        + [vm(10, 4, *tile)] * 6
         + [vm(*rim)] * 4
         + [vm(*sides)] * 2
         + [vm(*tile)] * 4

time: 18 us -> 16.6 us (0.922)
  the two profiles are of different devices: /device:TPU:5 before, /device:TPU:229 now
where the time goes in v4:
time: 16.6 us; the launch traced here: 16.5 us
  Pallas kernels  15.8 us (95%)
  local copies, waits for them, and re-layouts  0.71 us (4%)
    pallas_call x1, Pallas kernels, local(): pl.pallas_call(kernel, out_shape=pltpu.VMEM(cells, f32), in_specs=[pl.Blo...  15.8 us
    unnamed x1, local copies, waits for them, and re-layouts  0.71 us

profile of v4, /device:TPU:229, one launch (start us, length us, event | category | flops | bytes accessed | tf_op | source)
XLA Modules:
  0.0 16.5 jit_solution(15723846334055382738)
XLA Ops:
  0.0 15.8 %ocean.1 = f32[4,64,256]{2,1,0:T(8,128)S(1)} custom-call(f32[4,64,256]{2,1,0:T(8,128)} %tracer.1, f32[4,64,256]{2,1,0:T(8,128)} %diff.1, f32[4,64,256]{2,1,0:T(8,128)} %amp.1, f32[2,4,64,256]{3,2,1,0:T(8,128)} %noise_w.1, f32[2,4,64,256]{3,2,1,0:T(8,128)} %noise_z.1, s32[4,64,256]{2,1,0:T(8,128)} %land.1, s32[2048]{0:T(1024)} %partner.1), custom_call_target="tpu_custom_call" | custom-call | tf_op jit(solution)/shard_map/ocean/pallas_call | solution.py:768
  15.8 0.7 %copy.9 = f32[4,64,256]{2,1,0:T(8,128)} copy(f32[4,64,256]{2,1,0:T(8,128)S(1)} %ocean.1) | data formatting | bytes 524288

commit v5 on v4

--- a/solution.py
+++ b/solution.py
@@ -19,10 +19,10 @@
     tracer, diff, amp, noise_w, noise_z, land, partner, out,
     rx, rd, ra, rl, rw, rz, pc,
     xe, me, ge, he, ae, ke, x1, k2, we, ww, wy, wz, mp, mr, qe, so,
-    bx, bm, vn, vs, kr, x1r, k2r, x2r, bg, bh, ba, ve, vw, vz,
-    na, sa, nb, sb, em, wm, dne, dnw, dse, dsw, fa, fb,
+    bx, bm, vn, kr, x1r, k2r, x2r, bg, bh, ba, ve, vw, vz,
+    na, sa, nb, sb, em, wm, dne, dnw, dse, dsw, fa, fb, ga, gb,
     tn1, ts1, tn2, ts2, ep, wp, dn, ds,
-    isem, ssem, rsem, fsem_s, fsem_r,
+    isem, ssem, rsem, fsem_s, fsem_r, told,
 ):
     lat, lon, lev = lax.axis_index("lat"), lax.axis_index("lon"), lax.axis_index("lev")
     east, west = lax.rem(lon + 1, LON), lax.rem(lon + LON - 1, LON)
@@ -31,32 +31,37 @@
     at_fold = lat == LAT - 1
     own, theirs = NL * lev + 1, NL * other + 1
 
+    def beside(i):
+        return i + 1 - 2 * lax.rem(i, 2)
+
     bar = pltpu.get_barrier_semaphore()
 
     def greet(**where):
         pl.semaphore_signal(bar, inc=1, device_id=where, device_id_type=MESH)
 
+    late_row = lax.rem(lat, LAT // 2) // (LAT // 4)
+    fold_row, below_fold = (lat + 1) // LAT, (lat + 2) // LAT
+
     @pl.when(north_in)
     def _():
-        greet(lat=lat + 1)
-        greet(lat=lat + 1, lon=east)
-        greet(lat=lat + 1, lon=west)
-
-    @pl.when(south_in)
-    def _():
-        greet(lat=lat - 1)
-        greet(lat=lat - 1, lon=east)
-        greet(lat=lat - 1, lon=west)
-
-    greet(lon=east)
-    greet(lon=west)
+        for k in (lon, east, west):
+            greet(lat=lat + 1, lon=k, lev=1 - below_fold * other)
+
+    greet(lev=other)
+    for k in (east, west):
+        greet(lon=k, lev=late_row - fold_row * other)
 
     @pl.when(at_fold)
     def _():
+        greet(lon=beside(lon), lev=other)
         for k in (2, 4, 6):
             greet(lon=lax.rem(lon + k, LON))
-
-    greet(lev=other)
+            greet(lon=lax.rem(lon + k, LON), lev=other)
+
+    @pl.when(south_in)
+    def _():
+        for k in (lon, east, west):
+            greet(lat=lat - 1, lon=k, lev=0)
 
     loads = [
         pltpu.make_async_copy(s, d, isem.at[k])
@@ -98,15 +103,17 @@
         return pl.ds(pl.multiple_of(8 * r, 8), 8)
 
     for p in (0, 9):
+        for r in range(RT + 4):
+            sl = pl.ds(8 * r, 8)
+            bm[p, sl, :] = zero - 1.0
+            for ref in (bx, kr, x1r, k2r):
+                ref[p, sl, :] = zero
         for r in range(RT):
             sl = pl.ds(8 * r, 8)
             for lt in range(2):
                 me[p, lt, sl, :] = zero - 1.0
                 for ref in (xe, ke, x1, k2):
                     ref[p, lt, sl, :] = zero
-            bm[p, sl, :] = zero - 1.0
-            for ref in (bx, kr, x1r, k2r):
-                ref[p, sl, :] = zero
 
     @pl.when(lat == 0)
     def _():
@@ -231,19 +238,31 @@
         wp[i, 1] = where(halo_w, h, lroll(a, 4))
         return 0
 
-    early = lax.rem(lat, LAT // 2) < LAT // 4
+    early = late_row == 0
 
     @pl.when(early)
     def _():
         lax.fori_loop(0, NL, strips_second, 0)
 
-    @pl.when(lat == 0)
-    def _():
-        pl.semaphore_wait(bar, 6)
-
-    @pl.when(south_in)
-    def _():
-        pl.semaphore_wait(bar, 9)
+    def heard(when, count):
+        @pl.when(when)
+        def _():
+            pl.semaphore_wait(bar, count)
+
+    def tell():
+        pl.semaphore_signal(told, inc=1, device_id={"lev": other}, device_id_type=MESH)
+
+    heard(at_fold, 13)
+
+    @pl.when((lev == 0) & north_in)
+    def _():
+        heard(early, 11)
+        heard(jnp.logical_not(early), 7)
+        tell()
+
+    @pl.when((lev == 1) & north_in)
+    def _():
+        pl.semaphore_wait(told, 1)
 
     def send(k, src, dst, **where):
         return pltpu.make_async_remote_copy(
@@ -271,27 +290,36 @@
         send(9, wp, wm.at[mine], lon=east),
     ]
 
-    def beside(i):
-        return i + 1 - 2 * lax.rem(i, 2)
-
-    def fold_copy(ref, half, n, owner, target):
-        slot = ref.at[pl.ds(2 * owner, 2)]
+    def fold_copy(half, n, src, dst, **where):
         return pltpu.make_async_remote_copy(
-            src_ref=slot, dst_ref=slot, send_sem=fsem_s.at[half, n], recv_sem=fsem_r.at[half, n],
-            device_id={"lon": target}, device_id_type=MESH,
+            src_ref=src, dst_ref=dst, send_sem=fsem_s.at[half, n], recv_sem=fsem_r.at[half, n],
+            device_id=where, device_id_type=MESH,
         )
 
-    def fold_out(ref, half, n):
-        k = n if n < 4 else n - 3
-        target = beside(lon) if n == 0 else lax.rem(lon + 2 * k, LON)
-        return fold_copy(ref, half, n, lon if n < 4 else beside(lon), target)
-
-    def fold_in(ref, half, n):
-        k = n if n < 4 else n - 3
-        sender = beside(lon) if n == 0 else lax.rem(lon + LON - 2 * k, LON)
-        fold_copy(ref, half, n, sender if n < 4 else beside(sender), sender).wait_recv()
-
-    to_fold = [[fold_out(ref, half, n) for n in range(7)] for half, ref in enumerate((fa, fb))]
+    def block(half, owner):
+        return (fa, fb)[half].at[pl.ds(2 * owner, 2)]
+
+    def fold_out(half, n):
+        passed = (ga, gb)[half]
+        if n == 0:
+            return fold_copy(half, n, block(half, lon), passed, lon=beside(lon), lev=other)
+        if n < 4:
+            return fold_copy(half, n, block(half, lon), block(half, lon), lon=lax.rem(lon + 2 * n, LON))
+        to = block(half, beside(lon))
+        if n < 7:
+            return fold_copy(half, n, passed, to, lon=lax.rem(lon + 2 * n - 6, LON), lev=other)
+        return fold_copy(half, n, passed, to, lev=other)
+
+    def fold_in(half, n):
+        if n == 0:
+            part = (ga, gb)[half]
+        elif n < 4:
+            part = block(half, lax.rem(lon + LON - 2 * n, LON))
+        else:
+            part = block(half, beside(lax.rem(lon + LON + 6 - 2 * n, LON)) if n < 7 else beside(lon))
+        fold_copy(half, n, part, part, lev=other).wait_recv()
+
+    to_fold = [[fold_out(half, n) for n in range(8)] for half in range(2)]
 
     def planes(ref, start, count):
         return ref.at[pl.ds(start, count)]
@@ -303,13 +331,10 @@
     @pl.when(at_fold)
     def _():
         for half in to_fold:
-            for c in half[:4]:
+            half[0].start()
+        for half in to_fold:
+            for c in half[1:4]:
                 c.start()
-
-    @pl.when(south_in)
-    def _():
-        for k in (2, 3, 0, 1):
-            to_south[k].start()
 
     @pl.when(north_in)
     def _():
@@ -335,10 +360,33 @@
     @pl.when(jnp.logical_not(early))
     def _():
         lax.fori_loop(0, NL, strips_second, 0)
+
+    to_core[5].start()
+
+    def to_others():
+        @pl.when((lev == 0) & north_in)
+        def _():
+            pl.semaphore_wait(told, 1)
+
+        @pl.when((lev == 1) & north_in)
+        def _():
+            heard(jnp.logical_not(early), 11)
+            heard(early & south_in, 7)
+            heard(lat == 0, 1)
+            tell()
+
+        @pl.when(south_in)
+        def _():
+            for k in (2, 3, 0, 1):
+                to_south[k].start()
+
+    after = lax.rem(lat, LAT // 2) == 0
+    pl.when(jnp.logical_not(after))(to_others)
+
+    @pl.when(jnp.logical_not(early))
+    def _():
         for c in to_side:
             c.start()
-
-    to_core[5].start()
 
     def pair(ref, p, r):
         sl = pl.ds(8 * r, 8)
@@ -425,16 +473,16 @@
         p = own + i
         for ref, to in ((xe, bx), (me, bm)):
             for lt in range(2):
-                to[p, pl.ds(24 * lt, 8), :] = ref[p, lt, top, :]
-                to[p, pl.ds(24 * lt + 16, 8), :] = ref[p, lt, bottom, :]
+                to[p, pl.ds(24 + 24 * lt, 8), :] = ref[p, lt, top, :]
+                to[p, pl.ds(40 + 24 * lt, 8), :] = ref[p, lt, bottom, :]
         return 0
 
     lax.fori_loop(0, NL, copy_own, 0)
 
     @pl.when(at_fold)
     def _():
-        for half, ref in enumerate((fa, fb)):
-            fold_in(ref, half, 0)
+        for half in range(2):
+            fold_in(half, 0)
             for c in to_fold[half][4:]:
                 c.start()
 
@@ -449,8 +497,8 @@
                 me[p, lt, sl, :] = closed(mr[i, lt, sl, :])
         for ref, to in ((xe, bx), (me, bm)):
             for lt in range(2):
-                to[p, pl.ds(24 * lt, 8), :] = ref[p, lt, top, :]
-                to[p, pl.ds(24 * lt + 16, 8), :] = ref[p, lt, bottom, :]
+                to[p, pl.ds(24 + 24 * lt, 8), :] = ref[p, lt, top, :]
+                to[p, pl.ds(40 + 24 * lt, 8), :] = ref[p, lt, bottom, :]
         return 0
 
     lax.fori_loop(0, NL, close, 0)
@@ -468,6 +516,8 @@
     inner(x1, 1 + 3 * lev, 5, finish3)
     inner(k2, own, 4, finish4)
     share(15, so, NL * other, NL).wait_recv()
+
+    pl.when(after)(to_others)
 
     for c in to_side + to_core:
         c.wait_send()
@@ -529,9 +579,9 @@
             dst[NL * lev + i, 1] = v[1]
             dst[NL * lev + i, 2] = lroll(where(lo_half, v[0], v[3]), 116)
 
-    def fold_arrived(ref, half):
-        for n in range(1, 7):
-            fold_in(ref, half, n)
+    def fold_arrived(half):
+        for n in range(1, 8):
+            fold_in(half, n)
 
     @pl.when(north_in)
     def _():
@@ -541,7 +591,7 @@
 
     @pl.when(at_fold)
     def _():
-        fold_arrived(fa, 0)
+        fold_arrived(0)
         unfold(fa, na)
 
     relays[2].start()
@@ -568,9 +618,15 @@
             where(ring_w, v_w, where(halo_w, from_w, so[l, f, 1])),
         )
 
-    def put(ref, p, tiles, which):
+    def slot(k, shift=0):
+        return pl.ds((24, 32, 40, 48, 56, 64, 8, 80)[k] + shift, 8)
+
+    def put(ref, p, tiles, which, turned=True):
         for k, t in zip(which, tiles):
-            ref[p, pl.ds(8 * k, 8), :] = t
+            ref[p, slot(k), :] = t
+            if turned and k >= 6:
+                ref[p, slot(k, -8), :] = lroll(t, 12)
+                ref[p, slot(k, 8), :] = lroll(t, 116)
 
     fresh = (1, 4, 6, 7)
 
@@ -603,7 +659,10 @@
             bg[p, k], bh[p, k], ba[p, k] = g[k], h[k], a[k]
 
     def tiles(ref, p):
-        return [ref[p, pl.ds(8 * k, 8), :] for k in range(8)]
+        return [ref[p, slot(k), :] for k in range(8)]
+
+    def off(ref, p, d):
+        return [ref[p, slot(k, d), :] for k in range(8)]
 
     def rim_of(full, part, p):
         return [
@@ -620,39 +679,21 @@
         r = [lroll(t, 1) for t in v]
         return r[:3] + [where(lane == 0, r[k], r[k + 3]) for k in range(3)] + r[6:]
 
-    def strip_north(t):
-        r = sroll(t, 7)
-        return where(sub == 7, lroll(r, 116), r)
-
-    def strip_south(t):
-        r = sroll(t, 1)
-        return where(sub == 0, lroll(r, 12), r)
-
-    def rim_north(ref, p, v):
-        inside = [sroll(v[k], 7) if k % 3 == 2 else ref[p, pl.ds(8 * k + 1, 8), :] for k in range(6)]
-        return inside + [strip_north(t) for t in v[6:]]
-
-    def rim_south(ref, p, v):
-        inside = [sroll(v[k], 1) if k % 3 == 0 else ref[p, pl.ds(8 * k - 1, 8), :] for k in range(6)]
-        return inside + [strip_south(t) for t in v[6:]]
-
     every = range(8)
 
     def rim_weights(p):
-        m = tiles(bm, p)
-        e, n = rim_east(m), rim_north(bm, p, m)
-        w = [relu(m[k] + e[k]) for k in every]
-        v = rim_west(w)
-        for q, k in enumerate(fresh):
-            ve[p, q], vw[p, q] = w[k], v[k]
-        y = [relu(m[k] + n[k]) for k in every]
-        put(vn, p, y, every)
-        put(vs, p, rim_south(vn, p, y), every)
+        m, n = tiles(bm, p), off(bm, p, 1)
+        put(vn, p, [relu(m[k] + n[k]) for k in every], every)
+        b0, b1, t_e, t_w = (m[k] for k in fresh)
+        w = east_of([b0, b1]) + [lroll(t_e, 127), lroll(t_w, 127)]
+        w = [relu(m[k] + t) for k, t in zip(fresh, w)]
+        v = west_of(w[:2]) + [lroll(t, 1) for t in w[2:]]
+        for q in range(4):
+            ve[p, q], vw[p, q] = w[q], v[q]
 
     def rim_faces(p):
         for q, k in enumerate(fresh):
-            sl = pl.ds(8 * k, 8)
-            vz[p, q] = relu(0.5 * (bm[p, sl, :] + bm[p - 1, sl, :]))
+            vz[p, q] = relu(0.5 * (bm[p, slot(k), :] + bm[p - 1, slot(k), :]))
 
     def rim(u, base, count, finish):
         stack = [tiles(u, base + j) for j in range(-1, count + 1)]
@@ -665,9 +706,9 @@
         for j in range(count):
             p, here = base + j, stack[j + 1]
             fz_up = face(j + 1)
-            e, w, n, s = rim_east(here), rim_west(here), rim_north(u, p, here), rim_south(u, p, here)
+            e, w, n, s = rim_east(here), rim_west(here), off(u, p, 1), off(u, p, -1)
             we_, ww_ = rim_of(we, ve, p), rim_of(ww, vw, p)
-            wn_, ws_ = tiles(vn, p), tiles(vs, p)
+            wn_, ws_ = tiles(vn, p), off(vn, p, -1)
             finish(
                 p,
                 [
@@ -680,7 +721,7 @@
             fz = fz_up
 
     def rim1(p, total):
-        put(kr, p, [0.5 * t for t in total], every)
+        put(kr, p, [0.5 * t for t in total], every, False)
 
     def rim2(p, total):
         h = rim_of(he, bh, p)
@@ -692,7 +733,7 @@
 
     def rim4(p, total):
         x = tiles(x1r, p)
-        put(x2r, p, [x[k] + total[k] for k in every], every)
+        put(x2r, p, [x[k] + total[k] for k in every], every, False)
 
     def add_noise(p):
         g, k_ = rim_of(ge, bg, p), tiles(kr, p)
@@ -708,7 +749,7 @@
 
     @pl.when(at_fold)
     def _():
-        fold_arrived(fb, 1)
+        fold_arrived(1)
         unfold(fb, nb)
         relays[4].start()
 
@@ -777,12 +818,13 @@
         + [vm(*planes)] * 12
         + [vm(NL, 2, ROWS, 128)] * 3
         + [vm(2 * NL, 5, 2, *tile)]
-        + [vm(10, 64, 128)] * 8
+        + [vm(10, 96, 128)] * 7
         + [vm(10, 4, *tile)] * 6
         + [vm(*rim)] * 4
         + [vm(*sides)] * 2
         + [vm(*tile)] * 4
         + [vm(2 * LON, NL, *tile)] * 2
+        + [vm(2, NL, *tile)] * 2
         + [vm(*rows)] * 4
         + [vm(*rows)] * 2
         + [vm(*tile)] * 2
@@ -790,8 +832,9 @@
             pltpu.SemaphoreType.DMA((7,)),
             pltpu.SemaphoreType.DMA((22,)),
             pltpu.SemaphoreType.DMA((22,)),
-            pltpu.SemaphoreType.DMA((2, LON - 1)),
-            pltpu.SemaphoreType.DMA((2, LON - 1)),
+            pltpu.SemaphoreType.DMA((2, 8)),
+            pltpu.SemaphoreType.DMA((2, 8)),
+            pltpu.SemaphoreType.REGULAR,
         ],
         compiler_params=pltpu.CompilerParams(
             collective_id=0, has_side_effects=True, vmem_limit_bytes=VMEM

time: 16.6 us -> 16.2 us (0.976)
  Pallas kernels: 15.8 us -> 15.4 us
    pallas_call x1, Pallas kernels: 15.8 us -> 15.4 us  [local(): pl.pallas_call(kernel, out_shape=pltpu.VMEM(cells, f32), in_specs=[pl.Blo...]
where the time goes in v5:
time: 16.2 us; the launch traced here: 16.1 us
  Pallas kernels  15.4 us (95%)
  local copies, waits for them, and re-layouts  0.71 us (4%)
    pallas_call x1, Pallas kernels, local(): pl.pallas_call(kernel, out_shape=pltpu.VMEM(cells, f32), in_specs=[pl.Blo...  15.4 us
    unnamed x1, local copies, waits for them, and re-layouts  0.71 us

profile of v5, /device:TPU:229, one launch (start us, length us, event | category | flops | bytes accessed | tf_op | source)
XLA Modules:
  0.0 16.1 jit_solution(17132017488141818721)
XLA Ops:
  0.0 15.4 %ocean.1 = f32[4,64,256]{2,1,0:T(8,128)S(1)} custom-call(f32[4,64,256]{2,1,0:T(8,128)} %tracer.1, f32[4,64,256]{2,1,0:T(8,128)} %diff.1, f32[4,64,256]{2,1,0:T(8,128)} %amp.1, f32[2,4,64,256]{3,2,1,0:T(8,128)} %noise_w.1, f32[2,4,64,256]{3,2,1,0:T(8,128)} %noise_z.1, s32[4,64,256]{2,1,0:T(8,128)} %land.1, s32[2048]{0:T(1024)} %partner.1), custom_call_target="tpu_custom_call" | custom-call | tf_op jit(solution)/shard_map/ocean/pallas_call | solution.py:809
  15.4 0.7 %copy.9 = f32[4,64,256]{2,1,0:T(8,128)} copy(f32[4,64,256]{2,1,0:T(8,128)S(1)} %ocean.1) | data formatting | bytes 524288

commit v6 on v5

--- a/solution.py
+++ b/solution.py
@@ -121,6 +121,16 @@
             for lt in range(3):
                 sa[NL * lev + i, lt] = zero
                 sb[NL * lev + i, lt] = zero
+
+    last, last2 = 7 - 7 * lev, 6 - 5 * lev
+    for lt in range(3):
+        na[last, lt] = zero
+        sa[last, lt] = zero
+        nb[last2, lt] = zero
+        sb[last2, lt] = zero
+    for k in range(2):
+        em[last, k] = zero
+        wm[last, k] = zero
 
     for c in loads[:3]:
         c.wait()
@@ -538,14 +548,12 @@
             for c in half:
                 c.wait_send()
 
-    relays = [
-        share(16, em, NL * lev, NL),
-        share(17, wm, NL * lev, NL),
-        share(18, na, NL * lev, NL),
-        share(19, sa, NL * lev, NL),
-        share(20, nb, 1 + 3 * lev, 3),
-        share(21, sb, 1 + 3 * lev, 3),
-    ]
+    def next_levels(k, ref, l, count):
+        piece = ref.at[pl.ds(NL * l + (1 - l) * (NL - count), count)]
+        return send(k, piece, piece, lev=other)
+
+    halos = ((16, em, 3), (17, wm, 3), (18, na, 3), (19, sa, 3), (20, nb, 2), (21, sb, 2))
+    relays = [next_levels(k, ref, lev, count) for k, ref, count in halos]
     to_side[0].wait_recv()
     relays[0].start()
     to_side[1].wait_recv()
@@ -556,14 +564,6 @@
         for i in range(NL):
             one[NL * lev + i, 2] = lroll(d, at - 16 * i)
             half2[NL * lev + i, 2] = lroll(d, at - 16 * i - 8)
-
-    @pl.when(south_in)
-    def _():
-        for k in (0, 2, 3):
-            to_north[k].wait_recv()
-        corners(dsw, dse, 4, sa, sb)
-
-    relays[3].start()
 
     c0 = (pc[0] - COLS * lon) & (LON * COLS - 1)
     t0, shift = c0 >> 7, c0 & 127
@@ -585,27 +585,26 @@
 
     @pl.when(north_in)
     def _():
-        for k in (0, 2, 3):
+        for k in (0, 2, 3, 1):
             to_south[k].wait_recv()
         corners(dnw, dne, 112, na, nb)
+        relays[2].start()
+        relays[4].start()
+
+    @pl.when(south_in)
+    def _():
+        for k in (0, 2, 3, 1):
+            to_north[k].wait_recv()
+        corners(dsw, dse, 4, sa, sb)
+
+    relays[3].start()
+    relays[5].start()
 
     @pl.when(at_fold)
     def _():
         fold_arrived(0)
         unfold(fa, na)
-
-    relays[2].start()
-
-    @pl.when(south_in)
-    def _():
-        to_north[1].wait_recv()
-
-    relays[5].start()
-
-    @pl.when(north_in)
-    def _():
-        to_south[1].wait_recv()
-        relays[4].start()
+        relays[2].start()
 
     def ends(n, s):
         r = where(lo_half, lroll(both(s), 8), lroll(both(n), 116))
@@ -695,49 +694,47 @@
         for q, k in enumerate(fresh):
             vz[p, q] = relu(0.5 * (bm[p, slot(k), :] + bm[p - 1, slot(k), :]))
 
+    def mixed(full, part, p, k):
+        if k in fresh:
+            return part[p, fresh.index(k)]
+        return full[p, k // 3, top if k % 3 == 0 else bottom, :]
+
     def rim(u, base, count, finish):
-        stack = [tiles(u, base + j) for j in range(-1, count + 1)]
-
-        def face(j):
-            w = rim_of(wz, vz, base + j)
-            return [w[k] * (stack[j + 1][k] - stack[j][k]) for k in every]
-
-        fz = face(0)
-        for j in range(count):
-            p, here = base + j, stack[j + 1]
-            fz_up = face(j + 1)
-            e, w, n, s = rim_east(here), rim_west(here), off(u, p, 1), off(u, p, -1)
-            we_, ww_ = rim_of(we, ve, p), rim_of(ww, vw, p)
-            wn_, ws_ = tiles(vn, p), off(vn, p, -1)
-            finish(
-                p,
-                [
-                    (we_[k] * (e[k] - here[k]) - ww_[k] * (here[k] - w[k]))
-                    + (wn_[k] * (n[k] - here[k]) - ws_[k] * (here[k] - s[k]))
-                    + (fz_up[k] - fz[k])
-                    for k in every
-                ],
-            )
-            fz = fz_up
-
-    def rim1(p, total):
-        put(kr, p, [0.5 * t for t in total], every, False)
-
-    def rim2(p, total):
-        h = rim_of(he, bh, p)
-        put(x1r, p, [h[k] + total[k] for k in every], every)
-
-    def rim3(p, total):
-        a, x = rim_of(ae, ba, p), tiles(x1r, p)
-        put(k2r, p, [(x[k] + a[k]) + 0.5 * total[k] for k in every], every)
-
-    def rim4(p, total):
-        x = tiles(x1r, p)
-        put(x2r, p, [x[k] + total[k] for k in every], every, False)
+        for group in ((0, 3), (1, 4), (2, 5), (6,), (7,)):
+            pairs = len(group) == 2
+            stack = [[u[base + j, slot(k), :] for k in group] for j in range(-1, count + 1)]
+            faces = [
+                [mixed(wz, vz, base + j, k) * (hi - lo) for k, lo, hi in zip(group, stack[j], stack[j + 1])]
+                for j in range(count + 1)
+            ]
+            for j in range(count):
+                p, here = base + j, stack[j + 1]
+                e = east_of(here) if pairs else [lroll(here[0], 127)]
+                w = west_of(here) if pairs else [lroll(here[0], 1)]
+                for q, k in enumerate(group):
+                    c = here[q]
+                    total = (
+                        (mixed(we, ve, p, k) * (e[q] - c) - mixed(ww, vw, p, k) * (c - w[q]))
+                        + (vn[p, slot(k), :] * (u[p, slot(k, 1), :] - c) - vn[p, slot(k, -1), :] * (c - u[p, slot(k, -1), :]))
+                        + (faces[j + 1][q] - faces[j][q])
+                    )
+                    finish(p, k, total)
+
+    def rim1(p, k, total):
+        put(kr, p, [0.5 * total], (k,), False)
+
+    def rim2(p, k, total):
+        put(x1r, p, [mixed(he, bh, p, k) + total], (k,))
+
+    def rim3(p, k, total):
+        put(k2r, p, [(x1r[p, slot(k), :] + mixed(ae, ba, p, k)) + 0.5 * total], (k,))
+
+    def rim4(p, k, total):
+        if k not in (1, 4):
+            put(x2r, p, [x1r[p, slot(k), :] + total], (k,), False)
 
     def add_noise(p):
-        g, k_ = rim_of(ge, bg, p), tiles(kr, p)
-        put(kr, p, [g[k] + k_[k] for k in every], every)
+        put(kr, p, [mixed(ge, bg, p, k) + kr[p, slot(k), :] for k in every], every)
 
     for i in range(NL):
         place_first(NL * lev + i)
@@ -760,8 +757,8 @@
     rim(kr, 1 + 6 * lev, 2, rim2)
     rim(x1r, 1 + 7 * lev, 1, rim3)
 
-    for k, ref in ((16, em), (17, wm), (18, na), (19, sa)):
-        share(k, ref, NL * other, NL).wait_recv()
+    for k, ref, count in halos[:4]:
+        next_levels(k, ref, other, count).wait_recv()
     for i in range(NL):
         place_first(NL * other + i)
     for i in range(3):
@@ -769,8 +766,8 @@
     for i in range(NL):
         rim_faces(next_faces + i)
     rim(bx, near, 4, rim1)
-    share(20, nb, 1 + 3 * other, 3).wait_recv()
-    share(21, sb, 1 + 3 * other, 3).wait_recv()
+    for k, ref, count in halos[4:]:
+        next_levels(k, ref, other, count).wait_recv()
     for i in range(NL - 1):
         place_second(1 + 3 * other + i)
     for i in range(NL):
@@ -780,7 +777,7 @@
     rim(k2r, own, 4, rim4)
 
     for i in range(NL):
-        t = tiles(x2r, own + i)
+        t = {k: x2r[own + i, slot(k), :] for k in (0, 2, 3, 5, 6, 7)}
         edge = where(halo_w, t[6], t[7])
         for lt in range(2):
             cs = pl.ds(128 * lt, 128)

time: 16.2 us -> 16.2 us (level)
  no operation moved by 1% of the time
where the time goes in v6:
time: 16.2 us; the launch traced here: 16.1 us
  Pallas kernels  15.3 us (94%)
  local copies, waits for them, and re-layouts  0.71 us (4%)
    pallas_call x1, Pallas kernels, local(): pl.pallas_call(kernel, out_shape=pltpu.VMEM(cells, f32), in_specs=[pl.Blo...  15.3 us
    unnamed x1, local copies, waits for them, and re-layouts  0.71 us

profile of v6, /device:TPU:229, one launch (start us, length us, event | category | flops | bytes accessed | tf_op | source)
XLA Modules:
  0.0 16.1 jit_solution(1937315188098822584)
XLA Ops:
  0.0 15.3 %ocean.1 = f32[4,64,256]{2,1,0:T(8,128)S(1)} custom-call(f32[4,64,256]{2,1,0:T(8,128)} %tracer.1, f32[4,64,256]{2,1,0:T(8,128)} %diff.1, f32[4,64,256]{2,1,0:T(8,128)} %amp.1, f32[2,4,64,256]{3,2,1,0:T(8,128)} %noise_w.1, f32[2,4,64,256]{3,2,1,0:T(8,128)} %noise_z.1, s32[4,64,256]{2,1,0:T(8,128)} %land.1, s32[2048]{0:T(1024)} %partner.1), custom_call_target="tpu_custom_call" | custom-call | tf_op jit(solution)/shard_map/ocean/pallas_call | solution.py:806
  15.3 0.7 %copy.9 = f32[4,64,256]{2,1,0:T(8,128)} copy(f32[4,64,256]{2,1,0:T(8,128)S(1)} %ocean.1) | data formatting | bytes 524288

commit v7 on v6

--- a/solution.py
+++ b/solution.py
@@ -343,8 +343,8 @@
         for half in to_fold:
             half[0].start()
         for half in to_fold:
-            for c in half[1:4]:
-                c.start()
+            for n in (2, 1, 3):
+                half[n].start()
 
     @pl.when(north_in)
     def _():
@@ -493,8 +493,8 @@
     def _():
         for half in range(2):
             fold_in(half, 0)
-            for c in to_fold[half][4:]:
-                c.start()
+            for n in (5, 4, 6, 7):
+                to_fold[half][n].start()
 
     share(10, xe, theirs, NL).wait_recv()
     to_core[1].wait_recv()

time: 16.2 us -> 16 us (0.988)
    pallas_call x1, Pallas kernels: 15.3 us -> 15.2 us  [local(): pl.pallas_call(kernel, out_shape=pltpu.VMEM(cells, f32), in_specs=[pl.Blo...]
where the time goes in v7:
time: 16 us; the launch traced here: 15.9 us
  Pallas kernels  15.2 us (95%)
  local copies, waits for them, and re-layouts  0.71 us (4%)
    pallas_call x1, Pallas kernels, local(): pl.pallas_call(kernel, out_shape=pltpu.VMEM(cells, f32), in_specs=[pl.Blo...  15.2 us
    unnamed x1, local copies, waits for them, and re-layouts  0.71 us

profile of v7, /device:TPU:229, one launch (start us, length us, event | category | flops | bytes accessed | tf_op | source)
XLA Modules:
  0.0 15.9 jit_solution(7251393226852685312)
XLA Ops:
  0.0 15.2 %ocean.1 = f32[4,64,256]{2,1,0:T(8,128)S(1)} custom-call(f32[4,64,256]{2,1,0:T(8,128)} %tracer.1, f32[4,64,256]{2,1,0:T(8,128)} %diff.1, f32[4,64,256]{2,1,0:T(8,128)} %amp.1, f32[2,4,64,256]{3,2,1,0:T(8,128)} %noise_w.1, f32[2,4,64,256]{3,2,1,0:T(8,128)} %noise_z.1, s32[4,64,256]{2,1,0:T(8,128)} %land.1, s32[2048]{0:T(1024)} %partner.1), custom_call_target="tpu_custom_call" | custom-call | tf_op jit(solution)/shard_map/ocean/pallas_call | solution.py:806
  15.2 0.7 %copy.9 = f32[4,64,256]{2,1,0:T(8,128)} copy(f32[4,64,256]{2,1,0:T(8,128)S(1)} %ocean.1) | data formatting | bytes 524288

commit v8 on v7

--- a/solution.py
+++ b/solution.py
@@ -738,17 +738,17 @@
 
     for i in range(NL):
         place_first(NL * lev + i)
-    for i in range(NL):
-        rim_weights(own + i)
-    for i in range(NL):
-        rim_faces(far + i)
-    rim(bx, far, 3, rim1)
-
     @pl.when(at_fold)
     def _():
         fold_arrived(1)
         unfold(fb, nb)
         relays[4].start()
+
+    for i in range(NL):
+        rim_weights(own + i)
+    for i in range(NL):
+        rim_faces(far + i)
+    rim(bx, far, 3, rim1)
 
     for i in range(NL):
         place_second(NL * lev + i)

time: 16 us -> 16 us (level)
  no operation moved by 1% of the time
where the time goes in v8:
time: 16 us; the launch traced here: 15.9 us
  Pallas kernels  15.2 us (95%)
  local copies, waits for them, and re-layouts  0.71 us (4%)
    pallas_call x1, Pallas kernels, local(): pl.pallas_call(kernel, out_shape=pltpu.VMEM(cells, f32), in_specs=[pl.Blo...  15.2 us
    unnamed x1, local copies, waits for them, and re-layouts  0.71 us

profile of v8, /device:TPU:229, one launch (start us, length us, event | category | flops | bytes accessed | tf_op | source)
XLA Modules:
  0.0 15.9 jit_solution(14662088210153930066)
XLA Ops:
  0.0 15.2 %ocean.1 = f32[4,64,256]{2,1,0:T(8,128)S(1)} custom-call(f32[4,64,256]{2,1,0:T(8,128)} %tracer.1, f32[4,64,256]{2,1,0:T(8,128)} %diff.1, f32[4,64,256]{2,1,0:T(8,128)} %amp.1, f32[2,4,64,256]{3,2,1,0:T(8,128)} %noise_w.1, f32[2,4,64,256]{3,2,1,0:T(8,128)} %noise_z.1, s32[4,64,256]{2,1,0:T(8,128)} %land.1, s32[2048]{0:T(1024)} %partner.1), custom_call_target="tpu_custom_call" | custom-call | tf_op jit(solution)/shard_map/ocean/pallas_call | solution.py:806
  15.2 0.7 %copy.9 = f32[4,64,256]{2,1,0:T(8,128)} copy(f32[4,64,256]{2,1,0:T(8,128)S(1)} %ocean.1) | data formatting | bytes 524288

commit v9 on v8

--- a/solution.py
+++ b/solution.py
@@ -493,7 +493,7 @@
     def _():
         for half in range(2):
             fold_in(half, 0)
-            for n in (5, 4, 6, 7):
+            for n in (5, 6, 4, 7):
                 to_fold[half][n].start()
 
     share(10, xe, theirs, NL).wait_recv()

time: 16 us -> 16 us (level)
  no operation moved by 1% of the time
where the time goes in v9:
time: 16 us; the launch traced here: 15.9 us
  Pallas kernels  15.2 us (95%)
  local copies, waits for them, and re-layouts  0.71 us (4%)
    pallas_call x1, Pallas kernels, local(): pl.pallas_call(kernel, out_shape=pltpu.VMEM(cells, f32), in_specs=[pl.Blo...  15.2 us
    unnamed x1, local copies, waits for them, and re-layouts  0.71 us

profile of v9, /device:TPU:229, one launch (start us, length us, event | category | flops | bytes accessed | tf_op | source)
XLA Modules:
  0.0 15.9 jit_solution(2038576081979955458)
XLA Ops:
  0.0 15.2 %ocean.1 = f32[4,64,256]{2,1,0:T(8,128)S(1)} custom-call(f32[4,64,256]{2,1,0:T(8,128)} %tracer.1, f32[4,64,256]{2,1,0:T(8,128)} %diff.1, f32[4,64,256]{2,1,0:T(8,128)} %amp.1, f32[2,4,64,256]{3,2,1,0:T(8,128)} %noise_w.1, f32[2,4,64,256]{3,2,1,0:T(8,128)} %noise_z.1, s32[4,64,256]{2,1,0:T(8,128)} %land.1, s32[2048]{0:T(1024)} %partner.1), custom_call_target="tpu_custom_call" | custom-call | tf_op jit(solution)/shard_map/ocean/pallas_call | solution.py:806
  15.2 0.7 %copy.9 = f32[4,64,256]{2,1,0:T(8,128)} copy(f32[4,64,256]{2,1,0:T(8,128)S(1)} %ocean.1) | data formatting | bytes 524288
